TPU v7x, 128 devices: a whole 4x4x4 slice. The times are simulated.
128 devices in a mesh: ex: 16 (over x, y_lo, core), tp: 8 (over y_hi, z).
Axes of the slice: x: 4, y: 4 (y_hi: 2, y_lo: 2; y = y_hi * 2 + y_lo), z: 4, core: 2. Of those that a mesh axis runs over, the one named last changes fastest.
Arguments:
- acts: bfloat16 [12288, 28672], P('ex', 'tp'), may hold values from -20000 to 20000, as said below
- grads: bfloat16 [12288, 8192], P('ex', 'tp'), may hold values from -20000 to 20000, as said below
Outputs:
- kernel: float32 [12288, 3, 768], P(('ex', 'tp'))
Inputs may be any that keep to these rules, and one draw needn't show every extreme that they name: `acts`: finite values of order one to some thousands; every row has nonzero entries. `grads`: finite values of order one to some thousands; every row has nonzero entries.
All inputs are finite; a program needn't handle non-finite values.
Results may differ from a plain program's by a relative error of at most 0.00063.
Values may be sent and summed in bfloat16 or wider, within the bound.
A program may use at most 128 MiB of HBM per device.

v0:
```python
import jax
import jax.numpy as jnp
from jax import lax
from jax.sharding import PartitionSpec as P

epsilon = 1e-06


def shifted(value, axis, by):
    peers = lax.axis_size(axis)
    return lax.ppermute(value, axis, [(i, (i + by) % peers) for i in range(peers)])


def dot_rows(left, right):
    return lax.dot_general(
        left, right, (((1,), (1,)), ((), ())), preferred_element_type=jnp.float32
    )


def pass_along(act_block, grad_block):
    return shifted((act_block, grad_block), "ex", 1)


def on_device(acts, grads):
    acts_wide = acts.astype(jnp.float32)
    grads_wide = grads.astype(jnp.float32)
    totals = lax.psum(
        (jnp.sum(acts_wide * acts_wide, axis=1), jnp.sum(grads_wide * grads_wide, axis=1)), "tp"
    )
    act_unit = (acts_wide / jnp.sqrt(totals[0] + epsilon)[:, None]).astype(jnp.bfloat16)
    grad_unit = (grads_wide / jnp.sqrt(totals[1] + epsilon)[:, None]).astype(jnp.bfloat16)
    near_act, near_grad = pass_along(act_unit, grad_unit)
    far_act, far_grad = pass_along(near_act, near_grad)
    partners = [(act_unit, grad_unit), (near_act, near_grad), (far_act, far_grad)]
    tile_list = [
        jnp.stack([dot_rows(act_unit, pair[0]), dot_rows(grad_unit, pair[1])], axis=1)
        for pair in partners
    ]
    summed = lax.psum_scatter(jnp.stack(tile_list, axis=2), "tp", scatter_dimension=0, tiled=True)
    kernel = summed[:, 0] * summed[:, 1]
    return kernel


def solution(mesh):
    placed = (P("ex", "tp"), P("ex", "tp"))
    return jax.shard_map(
        on_device,
        mesh=mesh,
        in_specs=placed,
        out_specs=P(("ex", "tp"), None, None),
        check_vma=False,
    )
```

profile of v0, /device:TPU:1, one launch (start us, length us, event | category | flops | bytes accessed | tf_op | source)
XLA Modules:
  0.0 404.2 jit_solution(5686871987033232444)
XLA Ops:
  6.5 0.0 copy-start
  6.5 0.0 reduce-scatter.2.cloned.1.call-start
  6.5 3.8 fusion
  10.4 0.0 copy-done
  10.4 0.4 fusion.2
  10.7 23.0 %all-reduce = (f32[768]{0:T(1024)S(1)}, f32[768]{0:T(1024)S(1)}) all-reduce(f32[768]{0:T(1024)S(1)} %fusion.2, f32[768]{0:T(1024)S(1)} %fusion), channel_id=1, replica_groups=mesh['ex'=16,'tp'=8] {'tp'}, use_global_device_ids=true, to_apply=%region_3.0 | all-reduce | flops 1536 | bytes 12288 | tf_op jit(solution)/shard_map/psum | solution.py:27
  33.7 4.4 %fusion.1 = bf16[768,3584]{1,0:T(8,128)(2,1)S(1)} fusion(bf16[768,3584]{1,0:T(8,128)(2,1)} %param.2, f32[768]{0:T(1024)S(1)} %add_sqrt_fusion.1), kind=kLoop, calls=%fused_computation.4 | loop fusion | flops 8257536 | bytes 11013120 | tf_op jit(solution)/shard_map/convert_element_type | solution.py:30
  38.1 4.8 %collective-permute-start = (bf16[768,3584]{1,0:T(8,128)(2,1)S(1)}, bf16[768,3584]{1,0:T(8,128)(2,1)S(1)}, u32[]{:S(2)}, u32[]{:S(2)}) collective-permute-start(bf16[768,3584]{1,0:T(8,128)(2,1)S(1)} %fusion.1), channel_id=1, source_target_pairs={{0,8},{8,16},{16,24},{24,32},{32,40},{40,48},{48,56},{56,64},{64,7... | collective-permute-start | bytes 16515080 | tf_op jit(solution)/shard_map/ppermute | solution.py:11
  43.0 59.5 %collective-permute-done = bf16[768,3584]{1,0:T(8,128)(2,1)S(1)} collective-permute-done((bf16[768,3584]{1,0:T(8,128)(2,1)S(1)}, bf16[768,3584]{1,0:T(8,128)(2,1)S(1)}, u32[]{:S(2)}, u32[]{:S(2)}) %collective-permute-start) | collective-permute-done | bytes 5505056 | tf_op jit(solution)/shard_map/ppermute | solution.py:11
  102.5 2.5 collective-permute-start.2
  105.0 0.5 fusion.3
  105.5 0.1 collective-permute-start.1
  105.6 1.4 convolution_bitcast_fusion.2
  107.0 74.3 %collective-permute-done.1 = bf16[768,1024]{1,0:T(8,128)(2,1)S(1)} collective-permute-done((bf16[768,1024]{1,0:T(8,128)(2,1)S(1)}, bf16[768,1024]{1,0:T(8,128)(2,1)S(1)}, u32[]{:S(2)}, u32[]{:S(2)}) %collective-permute-start.1) | collective-permute-done | bytes 1572896 | tf_op jit(solution)/shard_map/ppermute | solution.py:11
  181.3 2.5 collective-permute-start.3
  183.8 4.4 %convolution_bitcast_fusion.5 = f32[768,1,768]{2,0,1:T(8,128)S(1)} fusion(bf16[768,3584]{1,0:T(8,128)(2,1)S(1)} %fusion.1), kind=kOutput, calls=%fused_computation.17 | convolution fusion | flops 4227858432 | bytes 7864320 | tf_op jit(solution)/shard_map/dot_general | solution.py:15
  188.2 2.6 maximum_bitcast_fusion
  190.8 1.4 convolution_bitcast_fusion.1
  192.2 8.9 %collective-permute-done.3 = bf16[768,1024]{1,0:T(8,128)(2,1)S(1)} collective-permute-done((bf16[768,1024]{1,0:T(8,128)(2,1)S(1)}, bf16[768,1024]{1,0:T(8,128)(2,1)S(1)}, u32[]{:S(2)}, u32[]{:S(2)}) %collective-permute-start.3) | collective-permute-done | bytes 1572896 | tf_op jit(solution)/shard_map/ppermute | solution.py:11
  201.2 1.4 convolution_bitcast_fusion
  202.6 4.4 %convolution_bitcast_fusion.4 = f32[768,1,768]{2,0,1:T(8,128)S(1)} fusion(bf16[768,3584]{1,0:T(8,128)(2,1)S(1)} %fusion.1, bf16[768,3584]{1,0:T(8,128)(2,1)S(1)} %collective-permute-done), kind=kOutput, calls=%fused_computation.16 | convolution fusion | flops 4227858432 | bytes 13369344 | tf_op jit(solution)/shard_map/dot_general | solution.py:15
  207.0 2.5 maximum_bitcast_fusion.1
  209.5 0.0 collective-permute-done.2
  209.5 4.4 %convolution_bitcast_fusion.3 = f32[768,1,768]{2,0,1:T(8,128)S(1)} fusion(bf16[768,3584]{1,0:T(8,128)(2,1)S(1)} %fusion.1, bf16[768,3584]{1,0:T(8,128)(2,1)S(1)} %collective-permute-done.2), kind=kOutput, calls=%fused_computation.15 | convolution fusion | flops 4227858432 | bytes 13369344 | tf_op jit(solution)/shard_map/dot_general | solution.py:15
  213.9 2.4 maximum_bitcast_fusion.2
  216.4 11.9 %pad_maximum_fusion = f32[768,2,3,768]{3,0,1,2:T(8,128)} fusion(f32[768,2,1,768]{3,0,1,2:T(8,128)} %maximum_bitcast_fusion.2, f32[768,2,1,768]{3,0,1,2:T(8,128)} %maximum_bitcast_fusion.1, f32[768,2,1,768]{3,0,1,2:T(8,128)} %maximum_bitcast_fusion), kind=kLoop, calls=%fused_computation | loop fusion | flops 7077888 | bytes 28311552 | tf_op jit(solution)/shard_map/stack | solution.py:39
  228.3 0.0 reduce-scatter.2.cloned.1.call-update
  228.3 166.6 %reduce-scatter.2.cloned.1.call-done = f32[96,2,3,768]{3,0,1,2:T(8,128)} async-done(((f32[768,2,3,768]{3,0,1,2:T(8,128)}), f32[96,2,3,768]{3,0,1,2:T(8,128)}) %reduce-scatter.2.cloned.1.call-update) | async-done | bytes 1769488 | tf_op jit(solution)/shard_map/reduce_scatter | solution.py:39
  395.0 2.4 fusion.4
  (2 shorter events, 0.0 us)
Async XLA Ops:
  6.5 3.8 copy-start
  6.5 388.4 %reduce-scatter.2.cloned.1.call-start = ((), (), s32[]{:S(2)}) async-start(), calls=%async_computation.1 | async-start | bytes 15925248 | tf_op jit(solution)/shard_map/reduce_scatter | solution.py:39
  38.1 64.3 %collective-permute-start = (bf16[768,3584]{1,0:T(8,128)(2,1)S(1)}, bf16[768,3584]{1,0:T(8,128)(2,1)S(1)}, u32[]{:S(2)}, u32[]{:S(2)}) collective-permute-start(bf16[768,3584]{1,0:T(8,128)(2,1)S(1)} %fusion.1), channel_id=1, source_target_pairs={{0,8},{8,16},{16,24},{24,32},{32,40},{40,48},{48,56},{56,64},{64,7... | collective-permute-start | bytes 16515080 | tf_op jit(solution)/shard_map/ppermute | solution.py:11
  102.5 107.0 %collective-permute-start.2 = (bf16[768,3584]{1,0:T(8,128)(2,1)S(1)}, bf16[768,3584]{1,0:T(8,128)(2,1)S(1)}, u32[]{:S(2)}, u32[]{:S(2)}) collective-permute-start(bf16[768,3584]{1,0:T(8,128)(2,1)S(1)} %collective-permute-done), channel_id=1, source_target_pairs={{0,8},{8,16},{16,24},{24,32},{32,40},{40,48},{48,56},{56,64},{64,7... | collective-permute-start | bytes 16515080 | tf_op jit(solution)/shard_map/ppermute | solution.py:11
  105.5 75.8 %collective-permute-start.1 = (bf16[768,1024]{1,0:T(8,128)(2,1)S(1)}, bf16[768,1024]{1,0:T(8,128)(2,1)S(1)}, u32[]{:S(2)}, u32[]{:S(2)}) collective-permute-start(bf16[768,1024]{1,0:T(8,128)(2,1)S(1)} %fusion.3), channel_id=1, source_target_pairs={{0,8},{8,16},{16,24},{24,32},{32,40},{40,48},{48,56},{56,64},{64,7... | collective-permute-start | bytes 4718600 | tf_op jit(solution)/shard_map/ppermute | solution.py:11
  181.3 19.8 %collective-permute-start.3 = (bf16[768,1024]{1,0:T(8,128)(2,1)S(1)}, bf16[768,1024]{1,0:T(8,128)(2,1)S(1)}, u32[]{:S(2)}, u32[]{:S(2)}) collective-permute-start(bf16[768,1024]{1,0:T(8,128)(2,1)S(1)} %collective-permute-done.1), channel_id=1, source_target_pairs={{0,8},{8,16},{16,24},{24,32},{32,40},{40,48},{48,56},{56,64},{64,7... | collective-permute-start | bytes 4718600 | tf_op jit(solution)/shard_map/ppermute | solution.py:11
Sparse Core Ops, SparseCore 0:
  228.5 166.4 reduce-scatter.1
where the time goes:
time: 404 us
  waiting for transfers between devices  309 us (76%)
  other arithmetic  31 us (8%)
  blocking collectives  23 us (6%)
  matrix products  17.6 us (4%)
  between operations  13.5 us (3%)
  starting transfers between devices  9.88 us (2%)
    reduce_scatter x1, waiting for transfers between devices, on_device(): lax.psum_scatter(jnp.stack(tile_list, axis=2), 'tp', scatter_dimension=0,...  167 us
    ppermute x4, waiting for transfers between devices, shifted(): lax.ppermute(value, axis, [(i, (i + by) % peers) for i in range(peers)])  143 us
    psum x1, blocking collectives, on_device(): lax.psum((jnp.sum(acts_wide * acts_wide, axis=1), jnp.sum(grads_wide * gr...  23 us
    another operation x4, other arithmetic, on_device(): jnp.stack(tile_list, axis=2)  19.4 us
    dot_general x6, matrix products, dot_rows(): lax.dot_general(left, right, (((1,), (1,)), ((), ())), preferred_element_...  17.6 us
    ppermute x4, starting transfers between devices, shifted(): lax.ppermute(value, axis, [(i, (i + by) % peers) for i in range(peers)])  9.88 us
  transfers between devices with their start and end apart: 5, of which 4 were waited for; matrix products, arithmetic and copies ran while one was open for 5% of the time, Pallas kernels for 0%

commit v1 on v0

v1 whole, which is shorter than its diff:
```python
import functools

import jax
import jax.numpy as jnp
from jax import lax
from jax.experimental import pallas as pl
from jax.experimental.pallas import tpu as pltpu
from jax.sharding import PartitionSpec as P

epsilon = 1e-06
MESH = pl.DeviceIdType.MESH
F32 = jnp.float32
BF16 = jnp.bfloat16

ROWS = 768
SEG = 96
KA, KG = 3584, 1024
HA, HG = KA // 2, KG // 2
NA, NG = 6, 2
CA, CG = ROWS // NA, ROWS // NG
WIDE = ROWS // 2

SCALE, SHIFT = 248.0, 124.0

UNITS = ["dg", "da", "wg", "wa", "c0g", "c1g", "c2g", "c0a", "c1a", "c2a"]
U = {name: i for i, name in enumerate(UNITS)}
SLOT = dict(dg=0, da=1, wg=2, wa=3, c0g=4, c1g=5, c2g=6, c0a=0, c1a=1, c2a=4)


def encode(value):
    power = jnp.exp2(jnp.abs(value) * SCALE - SHIFT)
    return jnp.where(value < 0, -power, power).astype(BF16)


def decode(code):
    wide = code.astype(F32)
    size = jnp.log(jnp.abs(wide)) * (1.4426950408889634 / SCALE) + SHIFT / SCALE
    return jnp.where(wide < 0, -size, size)


def dot_rows(left, right):
    return lax.dot_general(
        left, right, (((1,), (1,)), ((), ())), preferred_element_type=F32
    )


def kernel(
    acts, grads, out, w_a, w_g,
    own_a, own_g, u_a, u_g, tmp, part, z1s, z2s, ys, z1r, z2r, yr, sums, inv,
    own_sem, pair_send_a, pair_send_g, ab_a, ab_g, x_send_a, x_send_g, x_recv_a, x_recv_g,
    c_send_a, c_send_g, c_recv_a, c_recv_g, w_send, w_recv, w_load,
    sum_send, sum_recv, inv_send, inv_recv,
    z1_send, z1_recv, z2_send, z2_recv, y_send, y_recv,
):
    ex, tp = lax.axis_index("ex"), lax.axis_index("tp")
    x, r, c = ex // 4, (ex // 2) % 2, ex % 2
    yh, z = tp // 4, tp % 4
    x_next, x_prev = (x + 1) % 4, (x + 3) % 4
    z_next, z_prev, z_far = (z + 1) % 4, (z + 3) % 4, (z + 2) % 4

    def dev(xx, rr, cc, hh=yh, zz=z):
        return (xx * 4 + rr * 2 + cc, hh * 4 + zz)

    def remote(src, dst, send, recv, device):
        return pltpu.make_async_remote_copy(
            src_ref=src, dst_ref=dst, send_sem=send, recv_sem=recv,
            device_id=device, device_id_type=MESH,
        )

    def arrived(ref, sem):
        pltpu.make_async_copy(ref, ref, sem).wait()

    barrier = pltpu.get_barrier_semaphore()

    def greet(device):
        pl.semaphore_signal(barrier, inc=1, device_id=device, device_id_type=MESH)

    for step in range(1, 8):
        greet((ex, (tp + step) % 8))
    for rr, cc in ((0, 1), (1, 0), (1, 1)):
        greet(dev(x, (r + rr) % 2, (c + cc) % 2))
        greet(dev(x, (r + rr) % 2, (c + cc) % 2, 1 - yh))
    for rr in range(2):
        for cc in range(2):
            greet(dev(x_prev, rr, cc))
    pl.semaphore_wait(barrier, 17)

    pair, mate, ahead = dev(x, 1 - r, c), dev(x, r, 1 - c), dev(x_next, r, c)
    col_a = pl.multiple_of(r * HA, 128), pl.multiple_of((1 - r) * HA, 128)
    col_g = pl.multiple_of(r * HG, 128), pl.multiple_of((1 - r) * HG, 128)
    pltpu.make_async_copy(acts, own_a, own_sem.at[0]).start()
    pltpu.make_async_copy(grads, own_g, own_sem.at[1]).start()

    kinds = {
        0: (grads, u_g, col_g, HG, CG, NG, pair_send_g, ab_g, x_send_g, x_recv_g, c_send_g, c_recv_g),
        1: (acts, u_a, col_a, HA, CA, NA, pair_send_a, ab_a, x_send_a, x_recv_a, c_send_a, c_recv_a),
    }

    def rows_of(kind, k):
        chunk = kinds[kind][4]
        return pl.ds(pl.multiple_of(k * chunk, chunk), chunk)

    def pair_copy(kind, k):
        src, slots, cols, half, _, _, send, recv = kinds[kind][:8]
        rows = rows_of(kind, k)
        return remote(src.at[rows, pl.ds(cols[1], half)], slots.at[r, rows], send.at[k], recv.at[r, k], pair)

    def keep_copy(kind, k):
        src, slots, cols, half, _, _, _, recv = kinds[kind][:8]
        rows = rows_of(kind, k)
        return pltpu.make_async_copy(src.at[rows, pl.ds(cols[0], half)], slots.at[r, rows], recv.at[r, k])

    def x_copy(kind, k, first):
        src, slots, cols, half = kinds[kind][:4]
        send, recv = kinds[kind][8:10]
        rows = rows_of(kind, k)
        source = src.at[rows, pl.ds(cols[0], half)] if first else slots.at[1, rows]
        return remote(source, slots.at[2, rows], send.at[k], recv.at[k], ahead)

    def c_copy(kind, k, which):
        src, slots, cols, half = kinds[kind][:4]
        send, recv = kinds[kind][10:12]
        rows = rows_of(kind, k)
        source = src.at[rows, pl.ds(cols[0], half)] if which == 0 else slots.at[which, rows]
        return remote(source, slots.at[3, rows], send.at[k], recv.at[k], mate)

    def send_first(kind, k):
        pair_copy(kind, k).start()
        keep_copy(kind, k).start()

        @pl.when(r == 1)
        def _():
            x_copy(kind, k, True).start()

            @pl.when(c == 0)
            def _():
                c_copy(kind, k, 0).start()

    for kind in (0, 1):
        @pl.loop(0, kinds[kind][5])
        def _(k):
            send_first(kind, k)

    def w_copies():
        return (
            remote(acts, w_a, w_send.at[0], w_recv.at[0], mate),
            remote(grads, w_g, w_send.at[1], w_recv.at[1], mate),
        )

    @pl.when(c == 0)
    def _():
        for copy in w_copies():
            copy.start()

    def pass_block(kind, k):
        slots, recv = kinds[kind][1], kinds[kind][7]
        rows = rows_of(kind, k)
        arrived(slots.at[1, rows], recv.at[1, k])

        @pl.when(r == 0)
        def _():
            x_copy(kind, k, False).start()

            @pl.when(c == 0)
            def _():
                c_copy(kind, k, 1).start()

        arrived(slots.at[0, rows], recv.at[0, k])

    def pass_far(kind, k):
        slots, recv = kinds[kind][1], kinds[kind][9]
        rows = rows_of(kind, k)
        arrived(slots.at[2, rows], recv.at[k])

        @pl.when(c == 1)
        def _():
            c_copy(kind, k, 2).start()

    def wait_mate(kind, k):
        slots, recv = kinds[kind][1], kinds[kind][11]
        arrived(slots.at[3, rows_of(kind, k)], recv.at[k])

    def put_sums(ref, row, width):
        @pl.loop(0, ROWS // 128)
        def _(i):
            rows = pl.ds(pl.multiple_of(i * 128, 128), 128)
            total = jnp.zeros((128, 128), F32)
            for j in range(width // 128):
                value = ref[rows, 128 * j : 128 * j + 128].astype(F32)
                total += value * value
            sums[tp, row : row + 1, rows] = jnp.sum(total.T, axis=0, keepdims=True)

    sums[tp] = jnp.zeros((8, ROWS), F32)
    arrived(own_g, own_sem.at[1])
    put_sums(own_g, 0, KG)
    arrived(own_a, own_sem.at[0])
    put_sums(own_a, 1, KA)

    def sum_copy(step):
        peer = (tp + step) % 8
        return remote(sums.at[tp], sums.at[tp], sum_send.at[step], sum_recv.at[tp], (ex, peer))

    for step in range(1, 8):
        sum_copy(step).start()
    for step in range(1, 8):
        source = (tp + step) % 8
        arrived(sums.at[source], sum_recv.at[source])
    total = sums[0]
    for i in range(1, 8):
        total += sums[i]
    mine = 2 * r + c
    inv[mine] = 1.0 / jnp.sqrt(total + epsilon)

    def inv_near():
        return [
            remote(inv.at[mine], inv.at[mine], inv_send.at[i], inv_recv.at[mine],
                   dev(x, (r + rr) % 2, (c + cc) % 2))
            for i, (rr, cc) in enumerate(((0, 1), (1, 0), (1, 1)))
        ]
    def inv_far():
        return [
            remote(inv.at[mine], inv.at[4 + c], inv_send.at[3 + 2 * rr + cc], inv_recv.at[4 + c],
                   dev(x_next, rr, cc))
            for rr in range(2) for cc in range(2)
        ]

    near = inv_near()
    for copy in near:
        copy.start()

    @pl.when(r == 1)
    def _():
        for copy in inv_far():
            copy.start()

    pass_block(0, 0)

    def scale_rows(src, dst, block, row, start, count, width):
        @pl.loop(0, count // 128)
        def _(i):
            rows = pl.ds(pl.multiple_of(i * 128, 128), 128)
            lanes = pl.ds(pl.multiple_of(start + i * 128, 128), 128)
            col = jnp.broadcast_to(inv[block, row : row + 1, lanes], (128, 128)).T
            for j in range(width // 128):
                cols = slice(128 * j, 128 * j + 128)
                dst[rows, cols] = (src[rows, cols].astype(F32) * col).astype(BF16)

    def put_cols(unit, left, right, n):
        for m in range(2):
            block = dot_rows(left[WIDE * m : WIDE * m + WIDE, :], right[...])
            part[SLOT[unit], 4 * m : 4 * m + 4, :, pl.ds(pl.multiple_of(n * 256, 256), 256)] = (
                block.reshape(4, SEG, 256)
            )

    def put_rows(unit, left, right, m):
        for n in range(3):
            block = dot_rows(left[...], right[256 * n : 256 * n + 256, :])
            part[SLOT[unit], pl.ds(4 * m, 4), :, 256 * n : 256 * n + 256] = block.reshape(4, SEG, 256)

    def z1_copies(unit):
        u, s = U[unit], SLOT[unit]
        return (
            remote(z1s.at[s, 0], z1r.at[u, 0], z1_send.at[u, 0], z1_recv.at[u, 0], (ex, yh * 4 + z_next)),
            remote(z1s.at[s, 1], z1r.at[u, 1], z1_send.at[u, 1], z1_recv.at[u, 1], (ex, yh * 4 + z_prev)),
        )

    def z2_copies(unit):
        u, s = U[unit], SLOT[unit]
        return (
            remote(z2s.at[s, 0], z2r.at[u, 0], z2_send.at[u, 0], z2_recv.at[u, 0], (ex, yh * 4 + z_next)),
            remote(z2s.at[s, 1], z2r.at[u, 1], z2_send.at[u, 1], z2_recv.at[u, 1], (ex, yh * 4 + z_prev)),
        )

    def blocks(body):
        @pl.loop(0, 6)
        def _(i):
            body(i // 3, pl.ds(pl.multiple_of((i % 3) * 32, 32), 32))

    def z1(unit):
        s = SLOT[unit]

        def body(h, rows):
            z1s[s, 0, h, rows] = encode(part[s, h * 4 + z_far, rows, :WIDE])
            z1s[s, 1, h, rows] = encode(part[s, h * 4 + z_far, rows, WIDE:])

        blocks(body)
        for copy in z1_copies(unit):
            copy.start()

    def z2(unit):
        u, s = U[unit], SLOT[unit]
        for i in range(2):
            arrived(z1r.at[u, i], z1_recv.at[u, i])

        def body(h, rows):
            z2s[s, 0, h, rows, :WIDE] = encode(part[s, h * 4 + z_next, rows, :WIDE] + decode(z1r[u, 0, h, rows]))
            z2s[s, 0, h, rows, WIDE:] = encode(part[s, h * 4 + z_next, rows, WIDE:])
            z2s[s, 1, h, rows, :WIDE] = encode(part[s, h * 4 + z_prev, rows, :WIDE])
            z2s[s, 1, h, rows, WIDE:] = encode(part[s, h * 4 + z_prev, rows, WIDE:] + decode(z1r[u, 1, h, rows]))

        blocks(body)
        for copy in z2_copies(unit):
            copy.start()

    def target(unit):
        if unit[0] == "d":
            return r, c, 8 + yh, yh == yh
        if unit[0] == "w":
            return r, c, 4 + yh, yh == yh
        source = r * 2 + yh
        if unit[:2] == "c0":
            return 0, c, source, r == 0
        if unit[:2] == "c1":
            return 1, c, source, r == 1
        return c, 0, 4 + source, jnp.logical_and(r == 0, c == 0)

    def y_copy(unit, h):
        u, s, kind = U[unit], SLOT[unit], int(unit[-1] == "a")
        rr, cc, slot, _ = target(unit)
        return remote(ys.at[s, h], yr.at[kind, slot], y_send.at[u, h], y_recv.at[kind, slot], dev(x, rr, cc, h))

    def here(unit, h):
        return jnp.logical_and(target(unit)[3], yh == h)

    def z3(unit):
        u, s, kind = U[unit], SLOT[unit], int(unit[-1] == "a")
        for i in range(2):
            arrived(z2r.at[u, i], z2_recv.at[u, i])

        slot = target(unit)[2]

        def body(h, rows):
            total = part[s, h * 4 + z, rows, :] + decode(z2r[u, 0, h, rows]) + decode(z2r[u, 1, h, rows])
            code = encode(total)
            stays = here(unit, h)

            @pl.when(stays)
            def _():
                yr[kind, slot, rows] = code

            @pl.when(jnp.logical_not(stays))
            def _():
                ys[s, h, rows] = code

        blocks(body)
        for h in range(2):
            @pl.when(jnp.logical_not(here(unit, h)))
            def _():
                y_copy(unit, h).start()

    def sent(unit):
        for copy in z1_copies(unit) + z2_copies(unit):
            copy.wait_send()
        for h in range(2):
            @pl.when(jnp.logical_not(here(unit, h)))
            def _():
                y_copy(unit, h).wait_send()

    for i in range(3):
        rr, cc = ((0, 1), (1, 0), (1, 1))[i]
        block = 2 * ((r + rr) % 2) + (c + cc) % 2
        arrived(inv.at[block], inv_recv.at[block])
    for block in (4, 5):
        arrived(inv.at[block], inv_recv.at[block])

    scale_rows(own_g, own_g, mine, 0, 0, ROWS, KG)
    scale_rows(own_a, own_a, mine, 1, 0, ROWS, KA)

    @pl.loop(0, 3)
    def _(n):
        rows = pl.ds(pl.multiple_of(n * 256, 256), 256)
        put_cols("dg", own_g, own_g.at[rows], n)
        put_cols("da", own_a, own_a.at[rows], n)

    z1("dg")
    z1("da")
    pass_block(0, 1)

    @pl.when(c == 1)
    def _():
        arrived(w_a, w_recv.at[0])
        arrived(w_g, w_recv.at[1])

        @pl.loop(0, 3)
        def _(n):
            rows = pl.ds(pl.multiple_of(n * 256, 256), 256)
            wide, narrow = tmp.at[pl.ds(0, 256)], tmp.at[pl.ds(0, 256), pl.ds(0, KG)]
            load = pltpu.make_async_copy(w_g.at[rows], narrow, w_load)
            load.start()
            load.wait()
            scale_rows(narrow, narrow, 2 * r, 0, n * 256, 256, KG)
            put_cols("wg", own_g, narrow, n)
            load = pltpu.make_async_copy(w_a.at[rows], wide, w_load)
            load.start()
            load.wait()
            scale_rows(wide, wide, 2 * r, 1, n * 256, 256, KA)
            put_cols("wa", own_a, wide, n)

        z1("wg")
        z1("wa")

    spans = {0: (u_g, HG, "g"), 1: (u_a, HA, "a")}
    inv_of = {1: 2 + c, 2: 4 + c, 3: 5 - 3 * c}

    def cols_tile(unit, kind, slot):
        slots, half, _ = spans[kind]

        @pl.loop(0, 3)
        def _(n):
            rows = pl.ds(pl.multiple_of(n * 256, 256), 256)
            right = tmp.at[pl.ds(0, 256), pl.ds(0, half)]
            scale_rows(slots.at[slot, rows], right, inv_of[slot], kind, n * 256, 256, half)
            put_cols(unit, slots.at[0], right, n)

    def rows_tile(unit, kind, slot):
        slots, half, _ = spans[kind]

        @pl.loop(0, 2)
        def _(m):
            rows = pl.ds(pl.multiple_of(m * WIDE, WIDE), WIDE)
            left = tmp.at[pl.ds(0, WIDE), pl.ds(0, half)]
            scale_rows(slots.at[slot, rows], left, inv_of[slot], kind, m * WIDE, WIDE, half)
            put_rows(unit, left, slots.at[0], m)

    def scale_a(kind, k):
        slots, half, _ = spans[kind]
        rows, count = rows_of(kind, k), kinds[kind][4]
        block = slots.at[0, rows]
        scale_rows(block, block, c, kind, k * count, count, half)

    def mate_tile(unit, kind):
        @pl.when(c == 0)
        def _():
            cols_tile(unit, kind, 3)

        @pl.when(c == 1)
        def _():
            rows_tile(unit, kind, 3)

    def step(k):
        pass_block(1, k)
        scale_a(1, k)
        if k:
            pass_far(1, k - 1)

    pass_far(0, 0)
    step(0)
    z2("dg")
    z2("da")
    scale_a(0, 0)
    scale_a(0, 1)
    rows_tile("c1g", 0, 1)
    z1("c1g")
    pass_far(0, 1)
    cols_tile("c0g", 0, 2)
    z1("c0g")
    step(1)
    for k in range(NG):
        wait_mate(0, k)
    mate_tile("c2g", 0)
    z1("c2g")
    z3("dg")
    z3("da")
    step(2)

    @pl.when(c == 1)
    def _():
        z2("wg")
        z2("wa")

    z2("c1g")
    z2("c0g")
    z2("c2g")
    step(3)

    @pl.when(c == 1)
    def _():
        z3("wg")
        z3("wa")

    z3("c1g")
    z3("c0g")
    step(4)
    z3("c2g")
    sent("dg")
    sent("da")
    sent("c0g")
    step(5)
    rows_tile("c1a", 1, 1)
    z1("c1a")
    pass_far(1, 5)
    cols_tile("c0a", 1, 2)
    z1("c0a")
    z2("c1a")
    for k in range(NA):
        wait_mate(1, k)
    mate_tile("c2a", 1)
    z1("c2a")
    z2("c0a")
    z3("c1a")
    z2("c2a")
    z3("c0a")
    z3("c2a")

    def collect(kind, slot, stored):
        @pl.when(jnp.logical_not(stored))
        def _():
            arrived(yr.at[kind, slot], y_recv.at[kind, slot])

    for kind in range(2):
        for slot in range(4):
            collect(kind, slot, slot == 2 * r + yh)
        for h in range(2):
            collect(kind, 8 + h, h == yh)
            collect(kind, 4 + h, jnp.logical_and(h == yh, 2 * r + c != 2))
            collect(kind, 6 + h, c == 1)

    def product(index, slots):
        @pl.loop(0, 3)
        def _(i):
            rows = pl.ds(pl.multiple_of(i * 32, 32), 32)
            grams = []
            for kind in range(2):
                gram = decode(yr[kind, slots[0], rows])
                for slot in slots[1:]:
                    gram += decode(yr[kind, slot, rows])
                grams.append(gram)
            out[index, rows] = grams[0] * grams[1]

    product(0, (8, 9))
    product(2, (0, 1, 2, 3))

    @pl.when(c == 0)
    def _():
        product(1, (4, 5, 6, 7))

    @pl.when(c == 1)
    def _():
        product(1, (4, 5))

    for kind in (0, 1):
        @pl.loop(0, kinds[kind][5])
        def _(k):
            pair_copy(kind, k).wait_send()
            x_copy(kind, k, False).wait_send()
            c_copy(kind, k, 1).wait_send()

    @pl.when(c == 0)
    def _():
        for copy in w_copies():
            copy.wait_send()

    for step_ in range(1, 8):
        sum_copy(step_).wait_send()
    for copy in near:
        copy.wait_send()

    @pl.when(r == 1)
    def _():
        for copy in inv_far():
            copy.wait_send()

    @pl.when(c == 1)
    def _():
        sent("wg")
        sent("wa")

    for unit in ("c1g", "c2g", "c0a", "c1a", "c2a"):
        sent(unit)


def on_device(acts, grads):
    dma = pltpu.SemaphoreType.DMA
    n = len(UNITS)
    slots = 7
    any_space = pl.BlockSpec(memory_space=pl.ANY)
    result = pl.pallas_call(
        kernel,
        out_shape=(
            jax.ShapeDtypeStruct((3, SEG, ROWS), F32),
            jax.ShapeDtypeStruct((ROWS, KA), BF16),
            jax.ShapeDtypeStruct((ROWS, KG), BF16),
        ),
        in_specs=[any_space, any_space],
        out_specs=(pl.BlockSpec(memory_space=pltpu.VMEM), any_space, any_space),
        scratch_shapes=[
            pltpu.VMEM((ROWS, KA), BF16),
            pltpu.VMEM((ROWS, KG), BF16),
            pltpu.VMEM((4, ROWS, HA), BF16),
            pltpu.VMEM((4, ROWS, HG), BF16),
            pltpu.VMEM((WIDE, KA), BF16),
            pltpu.VMEM((slots, 8, SEG, ROWS), F32),
            pltpu.VMEM((slots, 2, 2, SEG, WIDE), BF16),
            pltpu.VMEM((slots, 2, 2, SEG, ROWS), BF16),
            pltpu.VMEM((slots, 2, SEG, ROWS), BF16),
            pltpu.VMEM((n, 2, 2, SEG, WIDE), BF16),
            pltpu.VMEM((n, 2, 2, SEG, ROWS), BF16),
            pltpu.VMEM((2, 10, SEG, ROWS), BF16),
            pltpu.VMEM((8, 8, ROWS), F32),
            pltpu.VMEM((6, 8, ROWS), F32),
            dma((2,)), dma((NA,)), dma((NG,)), dma((2, NA)), dma((2, NG)),
            dma((NA,)), dma((NG,)), dma((NA,)), dma((NG,)),
            dma((NA,)), dma((NG,)), dma((NA,)), dma((NG,)),
            dma((2,)), dma((2,)), dma,
            dma((8,)), dma((8,)), dma((7,)), dma((6,)),
            dma((n, 2)), dma((n, 2)), dma((n, 2)), dma((n, 2)), dma((n, 2)), dma((2, 10)),
        ],
        compiler_params=pltpu.CompilerParams(
            collective_id=0, has_side_effects=True, vmem_limit_bytes=64 * 1024 * 1024 - 65536
        ),
        cost_estimate=pl.CostEstimate(
            flops=2 * 3 * ROWS * ROWS * (KA + KG), bytes_accessed=4 * ROWS * (KA + KG), transcendentals=0
        ),
    )(acts, grads)
    return jnp.transpose(result[0], (1, 0, 2))


def solution(mesh):
    placed = (P("ex", "tp"), P("ex", "tp"))
    return jax.shard_map(
        on_device,
        mesh=mesh,
        in_specs=placed,
        out_specs=P(("ex", "tp"), None, None),
        check_vma=False,
    )
```

time: 404 us -> 210 us (0.52)
  waiting for transfers between devices: 309 us -> 0 us
  Pallas kernels: 0 us -> 208 us
  other arithmetic: 31 us -> 0 us
  blocking collectives: 23 us -> 0 us
  matrix products: 17.6 us -> 0 us
  between operations: 13.5 us -> 0.01 us
  starting transfers between devices: 9.88 us -> 0 us
    pallas_call x0 -> x1, Pallas kernels: none -> 208 us  [on_device(): pl.pallas_call(kernel, out_shape=(jax.ShapeDtypeStruct((3, SEG, ROWS), F3...]
    reduce_scatter x1 -> x0, waiting for transfers between devices: 167 us -> none  [on_device(): lax.psum_scatter(jnp.stack(tile_list, axis=2), 'tp', scatter_dimension=0,...]
    ppermute x4 -> x0, waiting for transfers between devices: 143 us -> none  [shifted(): lax.ppermute(value, axis, [(i, (i + by) % peers) for i in range(peers)])]
    psum x1 -> x0, blocking collectives: 23 us -> none  [on_device(): lax.psum((jnp.sum(acts_wide * acts_wide, axis=1), jnp.sum(grads_wide * gr...]
    another operation x4 -> x0, other arithmetic: 19.4 us -> none  [on_device(): jnp.stack(tile_list, axis=2)]
    dot_general x6 -> x0, matrix products: 17.6 us -> none  [dot_rows(): lax.dot_general(left, right, (((1,), (1,)), ((), ())), preferred_element_...]
    ppermute x4 -> x0, starting transfers between devices: 9.88 us -> none  [shifted(): lax.ppermute(value, axis, [(i, (i + by) % peers) for i in range(peers)])]
    convert_element_type x2 -> x0, other arithmetic: 4.96 us -> none  [the longest x1 4.41 us: on_device(): (acts_wide / jnp.sqrt(totals[0] + epsilon)[:, None]).astype(jnp.bfloat16)]
  transfers between devices with their start and end apart: 5 -> 0, of which waited for: 4 -> 0; matrix products, arithmetic and copies ran while one was open for 5% -> 0% of each run, Pallas kernels for 0% -> 0%
where the time goes in v1:
time: 210 us
  Pallas kernels  208 us (99%)
  local copies, waits for them, and re-layouts  2.14 us (1%)
    pallas_call x1, Pallas kernels, on_device(): pl.pallas_call(kernel, out_shape=(jax.ShapeDtypeStruct((3, SEG, ROWS), F3...  208 us

profile of v1, /device:TPU:1, one launch (start us, length us, event | category | flops | bytes accessed | tf_op | source)
XLA Modules:
  0.0 209.8 jit_solution(17134862216063593937)
XLA Ops:
  0.0 207.6 %shard_map.28 = (f32[3,96,768]{2,1,0:T(8,128)}, bf16[768,3584]{1,0:T(8,128)(2,1)}, bf16[768,1024]{1,0:T(8,128)(2,1)}) custom-call(bf16[768,3584]{1,0:T(8,128)(2,1)} %acts.1, bf16[768,1024]{1,0:T(8,128)(2,1)} %grads.1), custom_call_target="tpu_custom_call" | custom-call | flops 16307453952 | bytes 14155776 | tf_op jit(solution)/shard_map/pallas_call | solution.py:577
  207.7 2.1 %copy.4 = f32[96,3,768]{2,0,1:T(8,128)} copy(f32[96,3,768]{2,0,1:T(8,128)} %bitcast.1) | data formatting | bytes 1769472

commit v2 on v1

v2 whole, which is shorter than its diff:
```python
import functools

import jax
import jax.numpy as jnp
from jax import lax
from jax.experimental import pallas as pl
from jax.experimental.pallas import tpu as pltpu
from jax.sharding import PartitionSpec as P

epsilon = 1e-06
MESH = pl.DeviceIdType.MESH
F32 = jnp.float32
BF16 = jnp.bfloat16

ROWS = 768
SEG = 96
KA, KG = 3584, 1024
HA, HG = KA // 2, KG // 2
NA, NG = 12, 4
WINDOW = 3
LAG = 3
CA, CG = ROWS // NA, ROWS // NG
WIDE = ROWS // 2

SCALE, SHIFT = 248.0, 124.0

UNITS = ["dg", "da", "wg", "wa", "c0g", "c1g", "c2g", "c0a", "c1a", "c2a"]
U = {name: i for i, name in enumerate(UNITS)}
SLOT = dict(dg=0, da=1, wg=2, wa=3, c0g=4, c1g=5, c2g=6, c0a=4, c1a=1, c2a=0)


def encode(value):
    power = jnp.exp2(jnp.abs(value) * SCALE - SHIFT)
    return jnp.where(value < 0, -power, power).astype(BF16)


def decode(code):
    wide = code.astype(F32)
    size = jnp.log(jnp.abs(wide)) * (1.4426950408889634 / SCALE) + SHIFT / SCALE
    return jnp.where(wide < 0, -size, size)


def dot_rows(left, right):
    return lax.dot_general(
        left, right, (((1,), (1,)), ((), ())), preferred_element_type=F32
    )


def kernel(
    acts, grads, out, w_a, w_g,
    own_a, own_g, u_a, u_g, tmp, part, z1s, z2s, ys, z1r, z2r, yr, sums, inv,
    own_sem, keep_sem, pair_send_a, pair_send_g, ab_a, ab_g, x_send_a, x_send_g, x_recv_a, x_recv_g,
    c_send_a, c_send_g, c_recv_a, c_recv_g, w_send, w_recv, w_load,
    sum_send, sum_recv, inv_send, inv_recv,
    z1_send, z1_recv, z2_send, z2_recv, y_send, y_recv,
):
    ex, tp = lax.axis_index("ex"), lax.axis_index("tp")
    x, r, c = ex // 4, (ex // 2) % 2, ex % 2
    yh, z = tp // 4, tp % 4
    x_next, x_prev = (x + 1) % 4, (x + 3) % 4
    z_next, z_prev, z_far = (z + 1) % 4, (z + 3) % 4, (z + 2) % 4

    def dev(xx, rr, cc, hh=yh, zz=z):
        return (xx * 4 + rr * 2 + cc, hh * 4 + zz)

    def remote(src, dst, send, recv, device):
        return pltpu.make_async_remote_copy(
            src_ref=src, dst_ref=dst, send_sem=send, recv_sem=recv,
            device_id=device, device_id_type=MESH,
        )

    def arrived(ref, sem):
        pltpu.make_async_copy(ref, ref, sem).wait()

    barrier = pltpu.get_barrier_semaphore()

    def greet(device):
        pl.semaphore_signal(barrier, inc=1, device_id=device, device_id_type=MESH)

    for step in range(1, 8):
        greet((ex, (tp + step) % 8))
    for rr, cc in ((0, 1), (1, 0), (1, 1)):
        greet(dev(x, (r + rr) % 2, (c + cc) % 2))
        greet(dev(x, (r + rr) % 2, (c + cc) % 2, 1 - yh))
    for rr in range(2):
        for cc in range(2):
            greet(dev(x_prev, rr, cc))
    pl.semaphore_wait(barrier, 17)

    pair, mate, ahead = dev(x, 1 - r, c), dev(x, r, 1 - c), dev(x_next, r, c)
    col_a = pl.multiple_of(r * HA, 128), pl.multiple_of((1 - r) * HA, 128)
    col_g = pl.multiple_of(r * HG, 128), pl.multiple_of((1 - r) * HG, 128)
    pltpu.make_async_copy(acts, own_a, own_sem.at[0]).start()
    pltpu.make_async_copy(grads, own_g, own_sem.at[1]).start()

    kinds = {
        0: (grads, u_g, col_g, HG, CG, NG, pair_send_g, ab_g, x_send_g, x_recv_g, c_send_g, c_recv_g),
        1: (acts, u_a, col_a, HA, CA, NA, pair_send_a, ab_a, x_send_a, x_recv_a, c_send_a, c_recv_a),
    }
    order = [(0, k) for k in range(NG)] + [(1, k) for k in range(NA)]

    def rows_of(kind, k):
        chunk = kinds[kind][4]
        return pl.ds(k * chunk if isinstance(k, int) else pl.multiple_of(k * chunk, chunk), chunk)

    def pair_copy(kind, k):
        src, slots, cols, half, _, _, send, recv = kinds[kind][:8]
        rows = rows_of(kind, k)
        return remote(src.at[rows, pl.ds(cols[1], half)], slots.at[r, rows], send.at[k], recv.at[k], pair)

    def keep_copy(kind):
        src, slots, cols, half = kinds[kind][:4]
        return pltpu.make_async_copy(src.at[:, pl.ds(cols[0], half)], slots.at[r], keep_sem.at[kind])

    def x_copy(kind, k, first):
        src, slots, cols, half = kinds[kind][:4]
        send, recv = kinds[kind][8:10]
        rows = rows_of(kind, k)
        source = src.at[rows, pl.ds(cols[0], half)] if first else slots.at[1, rows]
        return remote(source, slots.at[2, rows], send.at[k], recv.at[k], ahead)

    def c_copy(kind, k, which):
        src, slots, cols, half = kinds[kind][:4]
        send, recv = kinds[kind][10:12]
        rows = rows_of(kind, k)
        source = src.at[rows, pl.ds(cols[0], half)] if which == 0 else slots.at[which, rows]
        return remote(source, slots.at[3, rows], send.at[k], recv.at[k], mate)

    def launch(q):
        kind, k = order[q]
        pair_copy(kind, k).start()

        @pl.when(r == 1)
        def _():
            x_copy(kind, k, True).start()

    for q in range(WINDOW):
        launch(q)
    for kind in (0, 1):
        keep_copy(kind).start()

        @pl.when(jnp.logical_and(r == 1, c == 0))
        def _():
            @pl.loop(0, kinds[kind][5])
            def _(k):
                c_copy(kind, k, 0).start()

    def w_copies():
        return (
            remote(acts, w_a, w_send.at[0], w_recv.at[0], mate),
            remote(grads, w_g, w_send.at[1], w_recv.at[1], mate),
        )

    @pl.when(c == 0)
    def _():
        for copy in w_copies():
            copy.start()

    def serve(q):
        kind, k = order[q]
        slots, recv = kinds[kind][1], kinds[kind][7]
        rows = rows_of(kind, k)
        pair_copy(kind, k).wait_send()
        if q + WINDOW < len(order):
            launch(q + WINDOW)
        arrived(slots.at[1 - r, rows], recv.at[k])

        @pl.when(r == 0)
        def _():
            x_copy(kind, k, False).start()

            @pl.when(c == 0)
            def _():
                c_copy(kind, k, 1).start()

        if q >= LAG:
            pass_far(q - LAG)

    def pass_far(q):
        kind, k = order[q]
        slots, recv = kinds[kind][1], kinds[kind][9]
        rows = rows_of(kind, k)
        arrived(slots.at[2, rows], recv.at[k])

        @pl.when(c == 1)
        def _():
            c_copy(kind, k, 2).start()

    def wait_mate(kind, first, last):
        slots, recv = kinds[kind][1], kinds[kind][11]
        for k in range(first, last):
            arrived(slots.at[3, rows_of(kind, k)], recv.at[k])

    def put_sums(ref, row, width):
        @pl.loop(0, ROWS // 128)
        def _(i):
            rows = pl.ds(pl.multiple_of(i * 128, 128), 128)
            total = jnp.zeros((128, 128), F32)
            for j in range(width // 128):
                value = ref[rows, 128 * j : 128 * j + 128].astype(F32)
                total += value * value
            sums[tp, row : row + 1, rows] = jnp.sum(total.T, axis=0, keepdims=True)

    sums[tp] = jnp.zeros((8, ROWS), F32)
    arrived(own_g, own_sem.at[1])
    put_sums(own_g, 0, KG)
    arrived(own_a, own_sem.at[0])
    put_sums(own_a, 1, KA)

    def sum_copy(step):
        peer = (tp + step) % 8
        return remote(sums.at[tp], sums.at[tp], sum_send.at[step], sum_recv.at[tp], (ex, peer))

    for step in range(1, 8):
        sum_copy(step).start()
    serve(0)
    for step in range(1, 8):
        source = (tp + step) % 8
        arrived(sums.at[source], sum_recv.at[source])
    total = sums[0]
    for i in range(1, 8):
        total += sums[i]
    mine = 2 * r + c
    inv[mine] = 1.0 / jnp.sqrt(total + epsilon)

    def inv_near():
        return [
            remote(inv.at[mine], inv.at[mine], inv_send.at[i], inv_recv.at[mine],
                   dev(x, (r + rr) % 2, (c + cc) % 2))
            for i, (rr, cc) in enumerate(((0, 1), (1, 0), (1, 1)))
        ]
    def inv_far():
        return [
            remote(inv.at[mine], inv.at[4 + c], inv_send.at[3 + 2 * rr + cc], inv_recv.at[4 + c],
                   dev(x_next, rr, cc))
            for rr in range(2) for cc in range(2)
        ]

    near = inv_near()
    for copy in near:
        copy.start()

    @pl.when(r == 1)
    def _():
        for copy in inv_far():
            copy.start()

    serve(1)

    def scale_rows(src, dst, block, row, start, count, width):
        @pl.loop(0, count // 128)
        def _(i):
            rows = pl.ds(pl.multiple_of(i * 128, 128), 128)
            lanes = pl.ds(pl.multiple_of(start + i * 128, 128), 128)
            col = jnp.broadcast_to(inv[block, row : row + 1, lanes], (128, 128)).T
            for j in range(width // 128):
                cols = slice(128 * j, 128 * j + 128)
                dst[rows, cols] = (src[rows, cols].astype(F32) * col).astype(BF16)

    def put_cols(unit, left, right, n):
        for m in range(2):
            block = dot_rows(left[WIDE * m : WIDE * m + WIDE, :], right[...])
            part[SLOT[unit], 4 * m : 4 * m + 4, :, pl.ds(pl.multiple_of(n * 256, 256), 256)] = (
                block.reshape(4, SEG, 256)
            )

    def by_rows(unit):
        if unit[:2] == "c0":
            return 0
        if unit[:2] == "c1":
            return 1 - r
        if unit[:2] == "c2":
            return c * (1 - r)
        return 1

    def quarter(unit, i, d):
        flag = by_rows(unit)
        h = flag * i + (1 - flag) * d
        n = flag * d + (1 - flag) * i
        return h, pl.ds(pl.multiple_of(n * WIDE, WIDE), WIDE), n

    z_peers = (ex, yh * 4 + z_next), (ex, yh * 4 + z_prev)

    def z1_copies(unit, i):
        u, s = U[unit], SLOT[unit]
        return [
            remote(z1s.at[s, i, d], z1r.at[u, i, d], z1_send.at[u, i, d], z1_recv.at[u, i, d], z_peers[d])
            for d in range(2)
        ]

    def z2_copies(unit, i):
        u, s = U[unit], SLOT[unit]
        return [
            remote(z2s.at[s, i, d], z2r.at[u, i, d], z2_send.at[u, i, d], z2_recv.at[u, i, d], z_peers[d])
            for d in range(2)
        ]

    def blocks(body):
        @pl.loop(0, 3)
        def _(k):
            body(pl.ds(pl.multiple_of(k * 32, 32), 32))

    def z1(unit, i):
        s = SLOT[unit]

        def body(rows):
            for d in range(2):
                h, cols, _ = quarter(unit, i, d)
                z1s[s, i, d, rows] = encode(part[s, h * 4 + z_far, rows, cols])

        blocks(body)
        for copy in z1_copies(unit, i):
            copy.start()

    def z2(unit, i):
        u, s = U[unit], SLOT[unit]
        for d in range(2):
            arrived(z1r.at[u, i, d], z1_recv.at[u, i, d])

        def body(rows):
            for d in range(2):
                h, cols, _ = quarter(unit, i, d)
                for way, to in ((0, z_next), (1, z_prev)):
                    value = part[s, h * 4 + to, rows, cols]
                    if way == d:
                        value += decode(z1r[u, i, d, rows])
                    z2s[s, i, way, d, rows] = encode(value)

        blocks(body)
        for copy in z2_copies(unit, i):
            copy.start()

    def target(unit):
        if unit[0] == "d":
            return r, c, 8 + yh, yh == yh
        if unit[0] == "w":
            return r, c, 4 + yh, yh == yh
        source = r * 2 + yh
        if unit[:2] == "c0":
            return 0, c, source, r == 0
        if unit[:2] == "c1":
            return 1, c, source, r == 1
        return c, 0, 4 + source, jnp.logical_and(r == 0, c == 0)

    def here(unit, h):
        return jnp.logical_and(target(unit)[3], yh == h)

    def y_copy(unit, i, d):
        u, s, kind = U[unit], SLOT[unit], int(unit[-1] == "a")
        rr, cc, slot, _ = target(unit)
        h, cols, n = quarter(unit, i, d)
        return remote(
            ys.at[s, i, d], yr.at[kind, slot, n], y_send.at[u, i, d], y_recv.at[kind, slot, n],
            dev(x, rr, cc, h),
        )

    def z3(unit, i):
        u, s, kind = U[unit], SLOT[unit], int(unit[-1] == "a")
        for d in range(2):
            arrived(z2r.at[u, i, d], z2_recv.at[u, i, d])
        slot = target(unit)[2]

        def body(rows):
            for d in range(2):
                h, cols, n = quarter(unit, i, d)
                total = part[s, h * 4 + z, rows, cols]
                total += decode(z2r[u, i, 0, d, rows]) + decode(z2r[u, i, 1, d, rows])
                code = encode(total)
                stays = here(unit, h)

                @pl.when(stays)
                def _():
                    yr[kind, slot, n, rows] = code

                @pl.when(jnp.logical_not(stays))
                def _():
                    ys[s, i, d, rows] = code

        blocks(body)
        for d in range(2):
            @pl.when(jnp.logical_not(here(unit, quarter(unit, i, d)[0])))
            def _():
                y_copy(unit, i, d).start()

    def sent(unit):
        for i in range(2):
            for copy in z1_copies(unit, i) + z2_copies(unit, i):
                copy.wait_send()
            for d in range(2):
                @pl.when(jnp.logical_not(here(unit, quarter(unit, i, d)[0])))
                def _():
                    y_copy(unit, i, d).wait_send()

    def both(step, *units):
        for unit in units:
            for i in range(2):
                step(unit, i)

    def on_core(core, step, *units):
        @pl.when(c == core)
        def _():
            both(step, *units)

    for i in range(3):
        rr, cc = ((0, 1), (1, 0), (1, 1))[i]
        block = 2 * ((r + rr) % 2) + (c + cc) % 2
        arrived(inv.at[block], inv_recv.at[block])
    for block in (4, 5):
        arrived(inv.at[block], inv_recv.at[block])

    serve(2)
    scale_rows(own_g, own_g, mine, 0, 0, ROWS, KG)
    scale_rows(own_a, own_a, mine, 1, 0, ROWS, KA)
    serve(3)

    @pl.loop(0, 3)
    def _(n):
        rows = pl.ds(pl.multiple_of(n * 256, 256), 256)
        put_cols("dg", own_g, own_g.at[rows], n)
        put_cols("da", own_a, own_a.at[rows], n)

    both(z1, "dg", "da")
    serve(4)
    for kind in (0, 1):
        arrived(kinds[kind][1].at[r], keep_sem.at[kind])

    spans = {0: (u_g, HG), 1: (u_a, HA)}
    inv_of = {1: 2 + c, 2: 4 + c, 3: 5 - 3 * c}

    def half_rows(i):
        return pl.ds(i * WIDE if isinstance(i, int) else pl.multiple_of(i * WIDE, WIDE), WIDE)

    def tile(unit, i, slot, a_left):
        kind = int(unit[-1] == "a")
        slots, half = spans[kind]
        scaled = tmp.at[pl.ds(0, WIDE), pl.ds(0, half)]

        @pl.loop(0, 2)
        def _(j):
            h, cols, n = quarter(unit, i, j)
            side = n if a_left else h
            stale = j == 0 if a_left else jnp.logical_or(j == 0, by_rows(unit) == 0)

            @pl.when(stale)
            def _():
                scale_rows(slots.at[slot, half_rows(side)], scaled, inv_of[slot], kind, side * WIDE, WIDE, half)

            fixed = slots[0, half_rows(h if a_left else n), :]
            other = scaled[...]
            block = dot_rows(fixed, other) if a_left else dot_rows(other, fixed)
            part[SLOT[unit], pl.ds(4 * h, 4), :, cols] = block.reshape(4, SEG, WIDE)

    def scale_a(kind, i):
        slots, half = spans[kind]
        block = slots.at[0, half_rows(i)]
        scale_rows(block, block, c, kind, i * WIDE, WIDE, half)

    def tile_b(unit, i):
        tile(unit, i, 1, False)
        z1(unit, i)

    def tile_p(unit, i):
        tile(unit, i, 2, True)
        z1(unit, i)

    def tile_x(unit, i, core):
        tile(unit, i, 3, core == 0)
        z1(unit, i)

    scale_a(0, 0)
    scale_a(0, 1)
    both(tile_b, "c1g")
    serve(5)

    @pl.when(c == 1)
    def _():
        arrived(w_a, w_recv.at[0])
        arrived(w_g, w_recv.at[1])

        @pl.loop(0, 3)
        def _(n):
            rows = pl.ds(pl.multiple_of(n * 256, 256), 256)
            wide, narrow = tmp.at[pl.ds(0, 256)], tmp.at[pl.ds(0, 256), pl.ds(0, KG)]
            load = pltpu.make_async_copy(w_g.at[rows], narrow, w_load)
            load.start()
            load.wait()
            scale_rows(narrow, narrow, 2 * r, 0, n * 256, 256, KG)
            put_cols("wg", own_g, narrow, n)
            load = pltpu.make_async_copy(w_a.at[rows], wide, w_load)
            load.start()
            load.wait()
            scale_rows(wide, wide, 2 * r, 1, n * 256, 256, KA)
            put_cols("wa", own_a, wide, n)

        both(z1, "wg", "wa")

    serve(6)
    both(z2, "dg", "da")
    serve(7)
    both(tile_p, "c0g")
    wait_mate(0, 0, NG)
    for core in range(2):
        @pl.when(c == core)
        def _():
            for i in range(2):
                tile_x("c2g", i, core)

    both(z3, "dg", "da")
    serve(8)
    on_core(1, z2, "wg", "wa")
    both(z2, "c1g")
    sent("dg")
    sent("da")
    serve(9)

    scale_a(1, 0)

    @pl.when(r == 0)
    def _():
        scale_a(1, 1)

    tile_b("c1a", 0)
    both(z2, "c0g", "c2g")
    serve(10)
    on_core(1, z3, "wg", "wa")
    both(z3, "c1g", "c0g")
    serve(11)

    @pl.when(c == 1)
    def _():
        wait_mate(1, 0, NA // 2)

        @pl.when(r == 1)
        def _():
            wait_mate(1, NA // 2, NA)

        tile_x("c2a", 0, 1)

    both(z3, "c2g")
    sent("c0g")
    serve(12)
    z2("c1a", 0)

    @pl.when(r == 0)
    def _():
        tile_p("c0a", 0)

    serve(13)

    @pl.when(c == 0)
    def _():
        wait_mate(1, 0, NA // 2)

        @pl.when(r == 0)
        def _():
            tile_x("c2a", 0, 0)

    z3("c1a", 0)
    serve(14)

    @pl.when(c == 1)
    def _():
        z2("c2a", 0)

    @pl.when(r == 0)
    def _():
        z2("c0a", 0)

    serve(15)

    @pl.when(r == 1)
    def _():
        scale_a(1, 1)

    tile_b("c1a", 1)

    @pl.when(r == 1)
    def _():
        tile_p("c0a", 0)

        @pl.when(c == 0)
        def _():
            tile_x("c2a", 0, 0)

    @pl.when(c == 1)
    def _():
        @pl.when(r == 0)
        def _():
            wait_mate(1, NA // 2, NA)

        tile_x("c2a", 1, 1)
        z3("c2a", 0)

    z2("c1a", 1)

    @pl.when(r == 1)
    def _():
        z2("c0a", 0)

    for q in range(len(order) - LAG, len(order)):
        pass_far(q)
    tile_p("c0a", 1)

    @pl.when(c == 0)
    def _():
        z2("c2a", 0)

    z3("c0a", 0)

    @pl.when(c == 0)
    def _():
        wait_mate(1, NA // 2, NA)
        tile_x("c2a", 1, 0)
        z3("c2a", 0)

    z3("c1a", 1)
    z2("c0a", 1)
    z2("c2a", 1)
    z3("c0a", 1)
    z3("c2a", 1)

    def collect(kind, slot, stored):
        @pl.when(jnp.logical_not(stored))
        def _():
            for n in range(2):
                arrived(yr.at[kind, slot, n], y_recv.at[kind, slot, n])

    for kind in range(2):
        for slot in range(4):
            collect(kind, slot, slot == 2 * r + yh)
        for h in range(2):
            collect(kind, 8 + h, h == yh)
            collect(kind, 4 + h, jnp.logical_and(h == yh, 2 * r + c != 2))
            collect(kind, 6 + h, c == 1)

    def product(index, slots):
        @pl.loop(0, 3)
        def _(k):
            rows = pl.ds(pl.multiple_of(k * 32, 32), 32)
            for n in range(2):
                grams = []
                for kind in range(2):
                    gram = decode(yr[kind, slots[0], n, rows])
                    for slot in slots[1:]:
                        gram += decode(yr[kind, slot, n, rows])
                    grams.append(gram)
                out[index, rows, WIDE * n : WIDE * n + WIDE] = grams[0] * grams[1]

    product(0, (8, 9))
    product(2, (0, 1, 2, 3))

    @pl.when(c == 0)
    def _():
        product(1, (4, 5, 6, 7))

    @pl.when(c == 1)
    def _():
        product(1, (4, 5))

    for kind in (0, 1):
        @pl.loop(0, kinds[kind][5])
        def _(k):
            x_copy(kind, k, False).wait_send()
            c_copy(kind, k, 1).wait_send()

    @pl.when(c == 0)
    def _():
        for copy in w_copies():
            copy.wait_send()

    for step_ in range(1, 8):
        sum_copy(step_).wait_send()
    for copy in near:
        copy.wait_send()

    @pl.when(r == 1)
    def _():
        for copy in inv_far():
            copy.wait_send()

    @pl.when(c == 1)
    def _():
        sent("wg")
        sent("wa")

    for unit in ("c1g", "c2g", "c0a", "c1a", "c2a"):
        sent(unit)


def on_device(acts, grads):
    dma = pltpu.SemaphoreType.DMA
    n = len(UNITS)
    slots = 7
    any_space = pl.BlockSpec(memory_space=pl.ANY)
    result = pl.pallas_call(
        kernel,
        out_shape=(
            jax.ShapeDtypeStruct((3, SEG, ROWS), F32),
            jax.ShapeDtypeStruct((ROWS, KA), BF16),
            jax.ShapeDtypeStruct((ROWS, KG), BF16),
        ),
        in_specs=[any_space, any_space],
        out_specs=(pl.BlockSpec(memory_space=pltpu.VMEM), any_space, any_space),
        scratch_shapes=[
            pltpu.VMEM((ROWS, KA), BF16),
            pltpu.VMEM((ROWS, KG), BF16),
            pltpu.VMEM((4, ROWS, HA), BF16),
            pltpu.VMEM((4, ROWS, HG), BF16),
            pltpu.VMEM((WIDE, KA), BF16),
            pltpu.VMEM((slots, 8, SEG, ROWS), F32),
            pltpu.VMEM((slots, 2, 2, SEG, WIDE), BF16),
            pltpu.VMEM((slots, 2, 2, 2, SEG, WIDE), BF16),
            pltpu.VMEM((slots, 2, 2, SEG, WIDE), BF16),
            pltpu.VMEM((n, 2, 2, SEG, WIDE), BF16),
            pltpu.VMEM((n, 2, 2, 2, SEG, WIDE), BF16),
            pltpu.VMEM((2, 10, 2, SEG, WIDE), BF16),
            pltpu.VMEM((8, 8, ROWS), F32),
            pltpu.VMEM((6, 8, ROWS), F32),
            dma((2,)), dma((2,)), dma((NA,)), dma((NG,)), dma((NA,)), dma((NG,)),
            dma((NA,)), dma((NG,)), dma((NA,)), dma((NG,)),
            dma((NA,)), dma((NG,)), dma((NA,)), dma((NG,)),
            dma((2,)), dma((2,)), dma,
            dma((8,)), dma((8,)), dma((7,)), dma((6,)),
            dma((n, 2, 2)), dma((n, 2, 2)), dma((n, 2, 2)), dma((n, 2, 2)), dma((n, 2, 2)), dma((2, 10, 2)),
        ],
        compiler_params=pltpu.CompilerParams(
            collective_id=0, has_side_effects=True, vmem_limit_bytes=64 * 1024 * 1024 - 65536
        ),
        cost_estimate=pl.CostEstimate(
            flops=2 * 3 * ROWS * ROWS * (KA + KG), bytes_accessed=4 * ROWS * (KA + KG), transcendentals=0
        ),
    )(acts, grads)
    return jnp.transpose(result[0], (1, 0, 2))


def solution(mesh):
    placed = (P("ex", "tp"), P("ex", "tp"))
    return jax.shard_map(
        on_device,
        mesh=mesh,
        in_specs=placed,
        out_specs=P(("ex", "tp"), None, None),
        check_vma=False,
    )
```

time: 210 us -> 153 us (0.73); the launches traced: 210 us -> 150 us
  Pallas kernels: 208 us -> 148 us
    pallas_call x1, Pallas kernels: 208 us -> 148 us  [on_device(): pl.pallas_call(kernel, out_shape=(jax.ShapeDtypeStruct((3, SEG, ROWS), F3...]
where the time goes in v2:
time: 153 us; the launch traced here: 150 us
  Pallas kernels  148 us (97%)
  local copies, waits for them, and re-layouts  2.14 us (1%)
    pallas_call x1, Pallas kernels, on_device(): pl.pallas_call(kernel, out_shape=(jax.ShapeDtypeStruct((3, SEG, ROWS), F3...  148 us

profile of v2, /device:TPU:1, one launch (start us, length us, event | category | flops | bytes accessed | tf_op | source)
XLA Modules:
  0.0 149.8 jit_solution(16850080822781458289)
XLA Ops:
  0.0 147.7 %shard_map.28 = (f32[3,96,768]{2,1,0:T(8,128)}, bf16[768,3584]{1,0:T(8,128)(2,1)}, bf16[768,1024]{1,0:T(8,128)(2,1)}) custom-call(bf16[768,3584]{1,0:T(8,128)(2,1)} %acts.1, bf16[768,1024]{1,0:T(8,128)(2,1)} %grads.1), custom_call_target="tpu_custom_call" | custom-call | flops 16307453952 | bytes 14155776 | tf_op jit(solution)/shard_map/pallas_call | solution.py:695
  147.7 2.1 %copy.4 = f32[96,3,768]{2,0,1:T(8,128)} copy(f32[96,3,768]{2,0,1:T(8,128)} %bitcast.1) | data formatting | bytes 1769472

commit v3 on v0

v3 whole, which is shorter than its diff:
```python
import functools

import jax
import jax.numpy as jnp
from jax import lax
from jax.experimental import pallas as pl
from jax.experimental.pallas import tpu as pltpu
from jax.sharding import PartitionSpec as P

epsilon = 1e-06
MESH = pl.DeviceIdType.MESH
F32 = jnp.float32
BF16 = jnp.bfloat16

ROWS = 768
SEG = 96
KA, KG = 3584, 1024
HA, HG = KA // 2, KG // 2
NA, NG = 4, 1
CA, CG = ROWS // NA, ROWS // NG
WIDE = ROWS // 2

SCALE, SHIFT = 248.0, 124.0

UNITS = ["dg", "da", "wg", "wa", "c0g", "c1g", "c2g", "c0a", "c1a", "c2a"]
U = {name: i for i, name in enumerate(UNITS)}
SLOT = dict(dg=0, da=1, wg=2, wa=3, c0g=4, c1g=5, c2g=6, c0a=7, c1a=1, c2a=0)


def encode(value):
    power = jnp.exp2(jnp.abs(value) * SCALE - SHIFT)
    return jnp.where(value < 0, -power, power).astype(BF16)


def decode(code):
    wide = code.astype(F32)
    size = jnp.log(jnp.abs(wide)) * (1.4426950408889634 / SCALE) + SHIFT / SCALE
    return jnp.where(wide < 0, -size, size)


def dot_rows(left, right):
    return lax.dot_general(
        left, right, (((1,), (1,)), ((), ())), preferred_element_type=F32
    )


def kernel(
    acts, grads, out, w_a, w_g,
    own_a, own_g, u_a, u_g, tmp, part, z1s, z2s, ys, z1r, z2r, yr, sums, inv,
    own_sem, keep_sem, pair_send_a, pair_send_g, ab_a, ab_g, x_send_a, x_send_g, x_recv_a, x_recv_g,
    c_send_a, c_send_g, c_recv_a, c_recv_g, w_send, w_recv, w_load,
    sum_send, sum_recv, inv_send, inv_recv,
    z1_send, z1_recv, z2_send, z2_recv, y_send, y_recv,
):
    ex, tp = lax.axis_index("ex"), lax.axis_index("tp")
    x, r, c = ex // 4, (ex // 2) % 2, ex % 2
    yh, z = tp // 4, tp % 4
    x_next, x_prev = (x + 1) % 4, (x + 3) % 4
    z_next, z_prev, z_far = (z + 1) % 4, (z + 3) % 4, (z + 2) % 4

    def dev(xx, rr, cc, hh=yh, zz=z):
        return (xx * 4 + rr * 2 + cc, hh * 4 + zz)

    def remote(src, dst, send, recv, device):
        return pltpu.make_async_remote_copy(
            src_ref=src, dst_ref=dst, send_sem=send, recv_sem=recv,
            device_id=device, device_id_type=MESH,
        )

    def arrived(ref, sem):
        pltpu.make_async_copy(ref, ref, sem).wait()

    pltpu.make_async_copy(acts, own_a, own_sem.at[0]).start()
    pltpu.make_async_copy(grads, own_g, own_sem.at[1]).start()

    barrier = pltpu.get_barrier_semaphore()

    def greet(device):
        pl.semaphore_signal(barrier, inc=1, device_id=device, device_id_type=MESH)

    for step in range(1, 8):
        greet((ex, (tp + step) % 8))
    for rr, cc in ((0, 1), (1, 0), (1, 1)):
        greet(dev(x, (r + rr) % 2, (c + cc) % 2))
        greet(dev(x, (r + rr) % 2, (c + cc) % 2, 1 - yh))
    for cc in range(2):
        for hh in range(2):
            greet(dev(x_prev, r, cc, hh))
            greet(dev(x_next, r, cc, hh))
    pl.semaphore_wait(barrier, 21)

    pair, mate = dev(x, 1 - r, c), dev(x, r, 1 - c)
    aside = dev((x + 3 + 2 * r) % 4, r, c)
    col_a = pl.multiple_of(r * HA, 128), pl.multiple_of((1 - r) * HA, 128)
    col_g = pl.multiple_of(r * HG, 128), pl.multiple_of((1 - r) * HG, 128)

    kinds = {
        0: (grads, u_g, col_g, HG, CG, NG, pair_send_g, ab_g, x_send_g, x_recv_g, c_send_g, c_recv_g),
        1: (acts, u_a, col_a, HA, CA, NA, pair_send_a, ab_a, x_send_a, x_recv_a, c_send_a, c_recv_a),
    }

    def rows_of(kind, k):
        chunk = kinds[kind][4]
        return pl.ds(k * chunk if isinstance(k, int) else pl.multiple_of(k * chunk, chunk), chunk)

    def pair_copy(kind, k):
        src, slots, cols, half, _, _, send, recv = kinds[kind][:8]
        rows = rows_of(kind, k)
        return remote(src.at[rows, pl.ds(cols[1], half)], slots.at[r, rows], send.at[k], recv.at[k], pair)

    def keep_copy(kind):
        src, slots, cols, half = kinds[kind][:4]
        return pltpu.make_async_copy(src.at[:, pl.ds(cols[0], half)], slots.at[r], keep_sem.at[kind])

    def x_copy(kind, k):
        src, slots, cols, half = kinds[kind][:4]
        send, recv = kinds[kind][8:10]
        rows = rows_of(kind, k)
        return remote(src.at[rows, pl.ds(cols[0], half)], slots.at[2, rows], send.at[k], recv.at[k], aside)

    def c_copy(kind, k, which):
        src, slots, cols, half = kinds[kind][:4]
        send, recv = kinds[kind][10:12]
        rows = rows_of(kind, k)
        source = src.at[rows, pl.ds(cols[0], half)] if which == 0 else slots.at[which, rows]
        return remote(source, slots.at[3, rows], send.at[k], recv.at[k], mate)

    def launch(kind, k):
        pair_copy(kind, k).start()
        x_copy(kind, k).start()

    launch(0, 0)
    for kind in (0, 1):
        keep_copy(kind).start()

        @pl.when(jnp.logical_and(r == 1, c == 0))
        def _():
            for k in range(kinds[kind][5]):
                c_copy(kind, k, 0).start()

    def w_copies():
        return (
            remote(own_a, w_a, w_send.at[0], w_recv.at[0], mate),
            remote(own_g, w_g, w_send.at[1], w_recv.at[1], mate),
        )

    def land(kind, k):
        slots, pair_recv, x_recv = kinds[kind][1], kinds[kind][7], kinds[kind][9]
        rows = rows_of(kind, k)
        arrived(slots.at[1 - r, rows], pair_recv.at[k])

        @pl.when(r == 0)
        def _():
            c_copy(kind, k, 1).start()

        arrived(slots.at[2, rows], x_recv.at[k])

        @pl.when(jnp.logical_and(r == 1, c == 1))
        def _():
            c_copy(kind, k, 2).start()

    def wait_gone(kind, first, last):
        for k in range(first, last):
            c_copy(kind, k, 1).wait_send()

    def wait_mate(kind, first, last):
        slots, recv = kinds[kind][1], kinds[kind][11]
        for k in range(first, last):
            arrived(slots.at[3, rows_of(kind, k)], recv.at[k])

    def put_sums(ref, row, width):
        @pl.loop(0, ROWS // 128)
        def _(i):
            rows = pl.ds(pl.multiple_of(i * 128, 128), 128)
            total = jnp.zeros((128, 128), F32)
            for j in range(width // 128):
                value = ref[rows, 128 * j : 128 * j + 128].astype(F32)
                total += value * value
            sums[tp, row : row + 1, rows] = jnp.sum(total.T, axis=0, keepdims=True)

    sums[tp] = jnp.zeros((8, ROWS), F32)
    arrived(own_g, own_sem.at[1])
    put_sums(own_g, 0, KG)
    arrived(own_a, own_sem.at[0])
    put_sums(own_a, 1, KA)

    def sum_copy(step):
        peer = (tp + step) % 8
        return remote(sums.at[tp], sums.at[tp], sum_send.at[step], sum_recv.at[tp], (ex, peer))

    for step in range(1, 8):
        sum_copy(step).start()
    for step in range(1, 8):
        source = (tp + step) % 8
        arrived(sums.at[source], sum_recv.at[source])
    total = sums[0]
    for i in range(1, 8):
        total += sums[i]
    mine = 2 * r + c
    inv[mine] = 1.0 / jnp.sqrt(total + epsilon)

    def inv_near():
        return [
            remote(inv.at[mine], inv.at[mine], inv_send.at[i], inv_recv.at[mine],
                   dev(x, (r + rr) % 2, (c + cc) % 2))
            for i, (rr, cc) in enumerate(((0, 1), (1, 0), (1, 1)))
        ]
    def inv_far():
        return [
            remote(inv.at[mine], inv.at[4 + c], inv_send.at[3], inv_recv.at[4 + c],
                   dev((x + 3 + 2 * r) % 4, r, c)),
            remote(inv.at[mine], inv.at[4 + c], inv_send.at[4], inv_recv.at[4 + c],
                   dev((x + 3 + 2 * r) % 4, r, 1 - c)),
        ]

    near = inv_near()
    for copy in near + inv_far():
        copy.start()

    def scale_rows(src, dst, block, row, start, count, width):
        @pl.loop(0, count // 128)
        def _(i):
            rows = pl.ds(pl.multiple_of(i * 128, 128), 128)
            lanes = pl.ds(pl.multiple_of(start + i * 128, 128), 128)
            col = jnp.broadcast_to(inv[block, row : row + 1, lanes], (128, 128)).T
            for j in range(width // 128):
                cols = slice(128 * j, 128 * j + 128)
                dst[rows, cols] = (src[rows, cols].astype(F32) * col).astype(BF16)

    def by_rows(unit):
        if unit[:2] == "c1":
            return 1 - r
        if unit[:2] == "c2":
            return 1 - r * c
        return int(unit[0] != "w")

    def quarter(unit, p):
        i, d = p // 2, p % 2
        flag = by_rows(unit)
        h = flag * i + (1 - flag) * d
        n = flag * d + (1 - flag) * i
        return h, pl.ds(n * WIDE if isinstance(n, int) else pl.multiple_of(n * WIDE, WIDE), WIDE), n

    z_peers = (ex, yh * 4 + z_next), (ex, yh * 4 + z_prev)
    bands = pl.ds(0, SEG // 2), pl.ds(SEG // 2, SEG // 2)

    def z1_copies(unit, p):
        u, s = U[unit], SLOT[unit]
        return [
            remote(z1s.at[s, p, bands[d]], z1r.at[u, p, bands[d]], z1_send.at[u, p, d], z1_recv.at[u, p, d], z_peers[d])
            for d in range(2)
        ]

    def z2_copies(unit, p):
        u, s = U[unit], SLOT[unit]
        return [
            remote(z2s.at[s, p, d], z2r.at[u, p, d], z2_send.at[u, p, d], z2_recv.at[u, p, d], z_peers[d])
            for d in range(2)
        ]

    def z1(unit, p):
        s = SLOT[unit]
        h, cols, _ = quarter(unit, p)
        z1s[s, p] = encode(part[s, h * 4 + z_far, :, cols])
        for copy in z1_copies(unit, p):
            copy.start()

    def z2(unit, p):
        u, s = U[unit], SLOT[unit]
        h, cols, _ = quarter(unit, p)
        for d in range(2):
            arrived(z1r.at[u, p, bands[d]], z1_recv.at[u, p, d])
        for way, to in ((0, z_next), (1, z_prev)):
            z2s[s, p, way, bands[way]] = encode(
                part[s, h * 4 + to, bands[way], cols] + decode(z1r[u, p, bands[way]])
            )
            z2s[s, p, way, bands[1 - way]] = encode(part[s, h * 4 + to, bands[1 - way], cols])
        for copy in z2_copies(unit, p):
            copy.start()

    def target(unit):
        if unit[0] == "d":
            return x, r, c, 8 + yh, yh == yh
        if unit[0] == "w":
            return x, r, c, 4 + yh, yh == yh
        source = r * 2 + yh
        if unit[:2] == "c0":
            return (x + 1 - r) % 4, 0, c, source, yh != yh
        if unit[:2] == "c1":
            return x, 1, c, source, r == 1
        return (x + (1 - c) * (1 - r)) % 4, c, 0, 4 + source, yh != yh

    def here(unit, p):
        return jnp.logical_and(target(unit)[4], yh == quarter(unit, p)[0])

    def y_copy(unit, p):
        u, s, kind = U[unit], SLOT[unit], int(unit[-1] == "a")
        xx, rr, cc, slot, _ = target(unit)
        h, _, n = quarter(unit, p)
        return remote(
            ys.at[s, p], yr.at[kind, slot, n], y_send.at[u, p], y_recv.at[kind, slot, n], dev(xx, rr, cc, h)
        )

    def z3(unit, p):
        u, s, kind = U[unit], SLOT[unit], int(unit[-1] == "a")
        h, cols, n = quarter(unit, p)
        slot = target(unit)[3]
        for d in range(2):
            arrived(z2r.at[u, p, d], z2_recv.at[u, p, d])
        total = part[s, h * 4 + z, :, cols] + decode(z2r[u, p, 0]) + decode(z2r[u, p, 1])
        ys[s, p] = encode(total)
        stays = here(unit, p)

        @pl.when(stays)
        def _():
            yr[kind, slot, n] = ys[s, p]

        @pl.when(jnp.logical_not(stays))
        def _():
            y_copy(unit, p).start()

    def gone(unit, p):
        for copy in z1_copies(unit, p) + z2_copies(unit, p):
            copy.wait_send()

        @pl.when(jnp.logical_not(here(unit, p)))
        def _():
            y_copy(unit, p).wait_send()

    def span(step, unit, first=0, last=4):
        @pl.loop(first, last)
        def _(p):
            step(unit, p)

    def every(step, *units):
        for unit in units:
            span(step, unit)

    def on_core(core, step, *units):
        @pl.when(c == core)
        def _():
            every(step, *units)

    def half_rows(i):
        return pl.ds(i * WIDE if isinstance(i, int) else pl.multiple_of(i * WIDE, WIDE), WIDE)

    def put(unit, p, left, right):
        h, cols, _ = quarter(unit, p)
        block = dot_rows(left, right)
        part[SLOT[unit], pl.ds(4 * h, 4), :, cols] = block.reshape(4, SEG, WIDE)

    scale_rows(own_g, own_g, mine, 0, 0, ROWS, KG)
    scale_rows(own_a, own_a, mine, 1, 0, ROWS, KA)

    @pl.when(c == 0)
    def _():
        for copy in w_copies():
            copy.start()

    def own_quarter(unit, p):
        ref = own_a if unit == "da" else own_g
        put(unit, p, ref[half_rows(p // 2), :], ref[half_rows(p % 2), :])
        z1(unit, p)

    span(own_quarter, "da", 0, 2)
    pair_copy(0, 0).wait_send()
    launch(1, 0)
    launch(1, 1)
    span(own_quarter, "da", 2, 4)
    span(own_quarter, "dg")

    spans = {0: (u_g, HG), 1: (u_a, HA)}
    block_3 = 2 * c + (1 - c) * (3 + 2 * r)

    def sides(unit):
        if unit[:2] == "c0":
            return 2 * (1 - r), 1 + r
        if unit[:2] == "c1":
            return 1, 0
        return 3 * c + 2 * (1 - c) * (1 - r), 3 * (1 - c)

    def tile(unit, p):
        slots, half = spans[int(unit[-1] == "a")]
        left, right = sides(unit)
        h, _, n = quarter(unit, p)
        put(unit, p, slots[left, half_rows(h), :], slots[right, half_rows(n), :])
        z1(unit, p)

    def scale(kind, slot, i):
        slots, half = spans[kind]
        block = slots.at[slot, half_rows(i)]
        number = block_3 if isinstance(slot, int) and slot == 3 else c + 2 * slot
        scale_rows(block, block, number, kind, i * WIDE, WIDE, half)

    for i in range(3):
        rr, cc = ((0, 1), (1, 0), (1, 1))[i]
        block = 2 * ((r + rr) % 2) + (c + cc) % 2
        arrived(inv.at[block], inv_recv.at[block])
    for block in (4, 5):
        arrived(inv.at[block], inv_recv.at[block])
    for kind in (0, 1):
        arrived(kinds[kind][1].at[r], keep_sem.at[kind])
    land(0, 0)
    wait_gone(0, 0, NG)
    wait_mate(0, 0, NG)
    for slot in (r, 1 - r, 2, 3):
        for i in range(2):
            scale(0, slot, i)
    every(tile, "c1g", "c0g", "c2g")
    every(z2, "da", "dg")

    @pl.when(c == 1)
    def _():
        arrived(w_a, w_recv.at[0])
        arrived(w_g, w_recv.at[1])

        @pl.loop(0, 2)
        def _(i):
            narrow = tmp.at[:, pl.ds(0, KG)]
            for unit, source, ref, own in (("wg", w_g, narrow, own_g), ("wa", w_a, tmp, own_a)):
                load = pltpu.make_async_copy(source.at[half_rows(i)], ref, w_load)
                load.start()
                load.wait()

                @pl.loop(0, 2)
                def _(d):
                    put(unit, 2 * i + d, own[half_rows(d), :], ref[...])
                    z1(unit, 2 * i + d)

    every(z2, "c1g", "c0g")
    for i in range(2):
        scale(1, r, i)
    every(z2, "c2g")
    pair_copy(1, 0).wait_send()
    launch(1, 2)
    on_core(1, z2, "wg", "wa")
    every(z3, "da", "dg")
    every(gone, "da", "dg")

    land(1, 0)
    land(1, 1)
    launch(1, 3)
    wait_gone(1, 0, NA // 2)
    scale(1, 1 - r, 0)
    span(tile, "c1a", 0, 2)
    scale(1, 2, 0)
    span(tile, "c0a", 0, 1)
    wait_mate(1, 0, NA // 2)
    scale(1, 3, 0)

    @pl.when(c == 0)
    def _():
        span(tile, "c2a", 0, 1)

    @pl.when(c == 1)
    def _():
        @pl.when(r == 1)
        def _():
            wait_mate(1, NA // 2, NA)
            scale(1, 3, 1)

        span(tile, "c2a", 0, 2)

    every(z3, "c1g", "c0g", "c2g")
    span(z2, "c1a", 0, 2)
    span(z2, "c0a", 0, 1)

    @pl.when(c == 0)
    def _():
        span(z2, "c2a", 0, 1)

    @pl.when(c == 1)
    def _():
        span(z2, "c2a", 0, 2)

    on_core(1, z3, "wg", "wa")
    span(z3, "c1a", 0, 2)
    span(z3, "c0a", 0, 1)
    span(z3, "c2a", 0, 1)

    @pl.when(c == 1)
    def _():
        span(z3, "c2a", 1, 2)

    land(1, 2)
    land(1, 3)

    @pl.when(r == 0)
    def _():
        wait_gone(1, NA // 2, NA)

    scale(1, 1 - r, 1)
    span(tile, "c1a", 2, 4)

    @pl.when(r == 1)
    def _():
        wait_gone(1, NA // 2, NA)

    scale(1, 2, 1)
    span(tile, "c0a", 1, 4)
    span(z2, "c1a", 2, 4)

    @pl.when(jnp.logical_not(jnp.logical_and(r == 1, c == 1)))
    def _():
        wait_mate(1, NA // 2, NA)
        scale(1, 3, 1)

    @pl.when(c == 0)
    def _():
        span(tile, "c2a", 1, 2)

    span(tile, "c2a", 2, 4)
    span(z2, "c0a", 1, 4)
    span(z3, "c1a", 2, 4)

    @pl.when(c == 0)
    def _():
        span(z2, "c2a", 1, 2)

    span(z2, "c2a", 2, 4)
    span(z3, "c0a", 1, 4)

    @pl.when(c == 0)
    def _():
        span(z3, "c2a", 1, 2)

    span(z3, "c2a", 2, 4)

    def collect(kind, slot, stored):
        @pl.when(jnp.logical_not(stored))
        def _():
            for n in range(2):
                arrived(yr.at[kind, slot, n], y_recv.at[kind, slot, n])

    for kind in range(2):
        for slot in range(4):
            collect(kind, slot, jnp.logical_and(r == 1, slot == 2 + yh))
        for h in range(2):
            collect(kind, 8 + h, h == yh)
            collect(kind, 4 + h, jnp.logical_and(h == yh, c == 1))
            collect(kind, 6 + h, c == 1)

    def product(index, slots):
        @pl.loop(0, 3)
        def _(k):
            rows = pl.ds(pl.multiple_of(k * 32, 32), 32)
            for n in range(2):
                grams = []
                for kind in range(2):
                    gram = decode(yr[kind, slots[0], n, rows])
                    for slot in slots[1:]:
                        gram += decode(yr[kind, slot, n, rows])
                    grams.append(gram)
                out[index, rows, WIDE * n : WIDE * n + WIDE] = grams[0] * grams[1]

    product(0, (8, 9))
    product(2, (0, 1, 2, 3))

    @pl.when(c == 0)
    def _():
        product(1, (4, 5, 6, 7))

    @pl.when(c == 1)
    def _():
        product(1, (4, 5))

    for kind in (0, 1):
        @pl.loop(0, kinds[kind][5])
        def _(k):
            x_copy(kind, k).wait_send()

    for k in range(1, NA):
        pair_copy(1, k).wait_send()

    @pl.when(c == 0)
    def _():
        for copy in w_copies():
            copy.wait_send()

    for step_ in range(1, 8):
        sum_copy(step_).wait_send()
    for copy in near + inv_far():
        copy.wait_send()

    on_core(1, gone, "wa", "wg")
    every(gone, "c0g", "c1g", "c2g", "c0a", "c1a", "c2a")


def on_device(acts, grads):
    dma = pltpu.SemaphoreType.DMA
    n = len(UNITS)
    slots = 8
    any_space = pl.BlockSpec(memory_space=pl.ANY)
    result = pl.pallas_call(
        kernel,
        out_shape=(
            jax.ShapeDtypeStruct((3, SEG, ROWS), F32),
            jax.ShapeDtypeStruct((ROWS, KA), BF16),
            jax.ShapeDtypeStruct((ROWS, KG), BF16),
        ),
        in_specs=[any_space, any_space],
        out_specs=(pl.BlockSpec(memory_space=pltpu.VMEM), any_space, any_space),
        scratch_shapes=[
            pltpu.VMEM((ROWS, KA), BF16),
            pltpu.VMEM((ROWS, KG), BF16),
            pltpu.VMEM((4, ROWS, HA), BF16),
            pltpu.VMEM((4, ROWS, HG), BF16),
            pltpu.VMEM((WIDE, KA), BF16),
            pltpu.VMEM((slots, 8, SEG, ROWS), F32),
            pltpu.VMEM((slots, 4, SEG, WIDE), BF16),
            pltpu.VMEM((slots, 4, 2, SEG, WIDE), BF16),
            pltpu.VMEM((slots, 4, SEG, WIDE), BF16),
            pltpu.VMEM((n, 4, SEG, WIDE), BF16),
            pltpu.VMEM((n, 4, 2, SEG, WIDE), BF16),
            pltpu.VMEM((2, 10, 2, SEG, WIDE), BF16),
            pltpu.VMEM((8, 8, ROWS), F32),
            pltpu.VMEM((6, 8, ROWS), F32),
            dma((2,)), dma((2,)), dma((NA,)), dma((NG,)), dma((NA,)), dma((NG,)),
            dma((NA,)), dma((NG,)), dma((NA,)), dma((NG,)),
            dma((NA,)), dma((NG,)), dma((NA,)), dma((NG,)),
            dma((2,)), dma((2,)), dma,
            dma((8,)), dma((8,)), dma((5,)), dma((6,)),
            dma((n, 4, 2)), dma((n, 4, 2)), dma((n, 4, 2)), dma((n, 4, 2)), dma((n, 4)), dma((2, 10, 2)),
        ],
        compiler_params=pltpu.CompilerParams(
            collective_id=0, has_side_effects=True, vmem_limit_bytes=64 * 1024 * 1024 - 65536
        ),
        cost_estimate=pl.CostEstimate(
            flops=2 * 3 * ROWS * ROWS * (KA + KG), bytes_accessed=4 * ROWS * (KA + KG), transcendentals=0
        ),
    )(acts, grads)
    return jnp.transpose(result[0], (1, 0, 2))


def solution(mesh):
    placed = (P("ex", "tp"), P("ex", "tp"))
    return jax.shard_map(
        on_device,
        mesh=mesh,
        in_specs=placed,
        out_specs=P(("ex", "tp"), None, None),
        check_vma=False,
    )
```

time: 404 us -> 146 us (0.36)
  waiting for transfers between devices: 309 us -> 0 us
  Pallas kernels: 0 us -> 142 us
  other arithmetic: 31 us -> 0 us
  blocking collectives: 23 us -> 0 us
  matrix products: 17.6 us -> 0 us
  between operations: 13.5 us -> 0.01 us
  starting transfers between devices: 9.88 us -> 0 us
    reduce_scatter x1 -> x0, waiting for transfers between devices: 167 us -> none  [on_device(): lax.psum_scatter(jnp.stack(tile_list, axis=2), 'tp', scatter_dimension=0,...]
    ppermute x4 -> x0, waiting for transfers between devices: 143 us -> none  [shifted(): lax.ppermute(value, axis, [(i, (i + by) % peers) for i in range(peers)])]
    pallas_call x0 -> x1, Pallas kernels: none -> 142 us  [on_device(): pl.pallas_call(kernel, out_shape=(jax.ShapeDtypeStruct((3, SEG, ROWS), F3...]
    psum x1 -> x0, blocking collectives: 23 us -> none  [on_device(): lax.psum((jnp.sum(acts_wide * acts_wide, axis=1), jnp.sum(grads_wide * gr...]
    another operation x4 -> x0, other arithmetic: 19.4 us -> none  [on_device(): jnp.stack(tile_list, axis=2)]
    dot_general x6 -> x0, matrix products: 17.6 us -> none  [dot_rows(): lax.dot_general(left, right, (((1,), (1,)), ((), ())), preferred_element_...]
    ppermute x4 -> x0, starting transfers between devices: 9.88 us -> none  [shifted(): lax.ppermute(value, axis, [(i, (i + by) % peers) for i in range(peers)])]
    convert_element_type x2 -> x0, other arithmetic: 4.96 us -> none  [the longest x1 4.41 us: on_device(): (acts_wide / jnp.sqrt(totals[0] + epsilon)[:, None]).astype(jnp.bfloat16)]
  transfers between devices with their start and end apart: 5 -> 0, of which waited for: 4 -> 0; matrix products, arithmetic and copies ran while one was open for 5% -> 0% of each run, Pallas kernels for 0% -> 0%
where the time goes in v3:
time: 146 us; the launch traced here: 144 us
  Pallas kernels  142 us (97%)
  local copies, waits for them, and re-layouts  2.14 us (1%)
    pallas_call x1, Pallas kernels, on_device(): pl.pallas_call(kernel, out_shape=(jax.ShapeDtypeStruct((3, SEG, ROWS), F3...  142 us

profile of v3, /device:TPU:1, one launch (start us, length us, event | category | flops | bytes accessed | tf_op | source)
XLA Modules:
  0.0 144.2 jit_solution(16602768068118716283)
XLA Ops:
  0.0 142.1 %shard_map.28 = (f32[3,96,768]{2,1,0:T(8,128)}, bf16[768,3584]{1,0:T(8,128)(2,1)}, bf16[768,1024]{1,0:T(8,128)(2,1)}) custom-call(bf16[768,3584]{1,0:T(8,128)(2,1)} %acts.1, bf16[768,1024]{1,0:T(8,128)(2,1)} %grads.1), custom_call_target="tpu_custom_call" | custom-call | flops 16307453952 | bytes 14155776 | tf_op jit(solution)/shard_map/pallas_call | solution.py:594
  142.1 2.1 %copy.4 = f32[96,3,768]{2,0,1:T(8,128)} copy(f32[96,3,768]{2,0,1:T(8,128)} %bitcast.1) | data formatting | bytes 1769472

commit v4 on v3

--- a/solution.py
+++ b/solution.py
@@ -518,13 +518,6 @@
         span(z2, "c2a", 1, 2)
 
     span(z2, "c2a", 2, 4)
-    span(z3, "c0a", 1, 4)
-
-    @pl.when(c == 0)
-    def _():
-        span(z3, "c2a", 1, 2)
-
-    span(z3, "c2a", 2, 4)
 
     def collect(kind, slot, stored):
         @pl.when(jnp.logical_not(stored))
@@ -532,37 +525,63 @@
             for n in range(2):
                 arrived(yr.at[kind, slot, n], y_recv.at[kind, slot, n])
 
-    for kind in range(2):
-        for slot in range(4):
-            collect(kind, slot, jnp.logical_and(r == 1, slot == 2 + yh))
-        for h in range(2):
-            collect(kind, 8 + h, h == yh)
-            collect(kind, 4 + h, jnp.logical_and(h == yh, c == 1))
-            collect(kind, 6 + h, c == 1)
-
-    def product(index, slots):
+    def gram_sum(kind, slots, n, rows):
+        gram = decode(yr[kind, slots[0], n, rows])
+        for slot in slots[1:]:
+            gram += decode(yr[kind, slot, n, rows])
+        return gram
+
+    def fill(index, slots, kinds_in):
         @pl.loop(0, 3)
         def _(k):
             rows = pl.ds(pl.multiple_of(k * 32, 32), 32)
             for n in range(2):
-                grams = []
-                for kind in range(2):
-                    gram = decode(yr[kind, slots[0], n, rows])
-                    for slot in slots[1:]:
-                        gram += decode(yr[kind, slot, n, rows])
-                    grams.append(gram)
-                out[index, rows, WIDE * n : WIDE * n + WIDE] = grams[0] * grams[1]
-
-    product(0, (8, 9))
-    product(2, (0, 1, 2, 3))
-
-    @pl.when(c == 0)
-    def _():
-        product(1, (4, 5, 6, 7))
+                cols = slice(WIDE * n, WIDE * n + WIDE)
+                value = gram_sum(kinds_in[0], slots, n, rows)
+                if len(kinds_in) > 1:
+                    value *= gram_sum(kinds_in[1], slots, n, rows)
+                elif kinds_in[0] == 1:
+                    value *= out[index, rows, cols]
+                out[index, rows, cols] = value
+
+    for kind in range(2):
+        for h in range(2):
+            collect(kind, 8 + h, h == yh)
+    fill(0, (8, 9), (0, 1))
+    for slot in range(4):
+        collect(0, slot, jnp.logical_and(r == 1, slot == 2 + yh))
+    fill(2, (0, 1, 2, 3), (0,))
+
+    @pl.when(c == 0)
+    def _():
+        for slot in range(4, 8):
+            collect(0, slot, yh != yh)
+        fill(1, (4, 5, 6, 7), (0,))
 
     @pl.when(c == 1)
     def _():
-        product(1, (4, 5))
+        for kind in range(2):
+            for h in range(2):
+                collect(kind, 4 + h, h == yh)
+        fill(1, (4, 5), (0, 1))
+
+    span(z3, "c0a", 1, 4)
+
+    @pl.when(c == 0)
+    def _():
+        span(z3, "c2a", 1, 2)
+
+    span(z3, "c2a", 2, 4)
+
+    for slot in range(4):
+        collect(1, slot, jnp.logical_and(r == 1, slot == 2 + yh))
+    fill(2, (0, 1, 2, 3), (1,))
+
+    @pl.when(c == 0)
+    def _():
+        for slot in range(4, 8):
+            collect(1, slot, yh != yh)
+        fill(1, (4, 5, 6, 7), (1,))
 
     for kind in (0, 1):
         @pl.loop(0, kinds[kind][5])

time: 146 us -> 144 us (0.986)
  no operation moved by 1% of the time
where the time goes in v4:
time: 144 us; the launch traced here: 143 us
  Pallas kernels  141 us (98%)
  local copies, waits for them, and re-layouts  2.14 us (1%)
    pallas_call x1, Pallas kernels, on_device(): pl.pallas_call(kernel, out_shape=(jax.ShapeDtypeStruct((3, SEG, ROWS), F3...  141 us

profile of v4, /device:TPU:1, one launch (start us, length us, event | category | flops | bytes accessed | tf_op | source)
XLA Modules:
  0.0 143.2 jit_solution(7724391172178692144)
XLA Ops:
  0.0 141.1 %shard_map.28 = (f32[3,96,768]{2,1,0:T(8,128)}, bf16[768,3584]{1,0:T(8,128)(2,1)}, bf16[768,1024]{1,0:T(8,128)(2,1)}) custom-call(bf16[768,3584]{1,0:T(8,128)(2,1)} %acts.1, bf16[768,1024]{1,0:T(8,128)(2,1)} %grads.1), custom_call_target="tpu_custom_call" | custom-call | flops 16307453952 | bytes 14155776 | tf_op jit(solution)/shard_map/pallas_call | solution.py:613
  141.1 2.1 %copy.4 = f32[96,3,768]{2,0,1:T(8,128)} copy(f32[96,3,768]{2,0,1:T(8,128)} %bitcast.1) | data formatting | bytes 1769472

commit v5 on v4

--- a/solution.py
+++ b/solution.py
@@ -362,9 +362,9 @@
         put(unit, p, ref[half_rows(p // 2), :], ref[half_rows(p % 2), :])
         z1(unit, p)
 
+    launch(1, 0)
     span(own_quarter, "da", 0, 2)
     pair_copy(0, 0).wait_send()
-    launch(1, 0)
     launch(1, 1)
     span(own_quarter, "da", 2, 4)
     span(own_quarter, "dg")

time: 144 us -> 145 us (level)
  Pallas kernels: 141 us -> 143 us
    pallas_call x1, Pallas kernels: 141 us -> 143 us  [on_device(): pl.pallas_call(kernel, out_shape=(jax.ShapeDtypeStruct((3, SEG, ROWS), F3...]
where the time goes in v5:
time: 145 us
  Pallas kernels  143 us (99%)
  local copies, waits for them, and re-layouts  2.14 us (1%)
    pallas_call x1, Pallas kernels, on_device(): pl.pallas_call(kernel, out_shape=(jax.ShapeDtypeStruct((3, SEG, ROWS), F3...  143 us

profile of v5, /device:TPU:1, one launch (start us, length us, event | category | flops | bytes accessed | tf_op | source)
XLA Modules:
  0.0 145.0 jit_solution(17845237655820545266)
XLA Ops:
  0.0 142.9 %shard_map.28 = (f32[3,96,768]{2,1,0:T(8,128)}, bf16[768,3584]{1,0:T(8,128)(2,1)}, bf16[768,1024]{1,0:T(8,128)(2,1)}) custom-call(bf16[768,3584]{1,0:T(8,128)(2,1)} %acts.1, bf16[768,1024]{1,0:T(8,128)(2,1)} %grads.1), custom_call_target="tpu_custom_call" | custom-call | flops 16307453952 | bytes 14155776 | tf_op jit(solution)/shard_map/pallas_call | solution.py:613
  142.9 2.1 %copy.4 = f32[96,3,768]{2,0,1:T(8,128)} copy(f32[96,3,768]{2,0,1:T(8,128)} %bitcast.1) | data formatting | bytes 1769472
